TPU v7x, 128 devices: a whole 4x4x4 slice. The times are simulated.
128 devices in a mesh: seq: 32 (over z, y, core), head: 4 (over x).
Axes of the slice: x: 4, y: 4, z: 4, core: 2. Of those that a mesh axis runs over, the one named last changes fastest.
Arguments:
- tokens: bfloat16 [2, 8192, 2048], P(None, 'seq', 'head'), may hold values from -6 to 6
- lengths: int32 [2], replicated, may hold values from 2048 to 8192, as said below
- norm_gain: float32 [2048], replicated, may hold values from 0.25 to 1.75
- query_key_value_weight: bfloat16 [3, 2048, 2048], P(None, None, 'head'), may hold values from -0.125 to 0.125
- strength_projection: bfloat16 [2048, 16], P(None, 'head'), may hold values from -0.125 to 0.125
- conv_weight: float32 [3, 4, 2048], P(None, None, 'head'), may hold values from -3 to 3
- head_gain: float32 [128], replicated, may hold values from 0.25 to 1.75
- output_projection: bfloat16 [2048, 2048], P('head'), may hold values from -0.125 to 0.125
- mlp_gain: float32 [2048], replicated, may hold values from 0.25 to 1.75
- gate_up_weight: bfloat16 [2, 2048, 5632], P(None, None, 'head'), may hold values from -0.125 to 0.125
- down_projection: bfloat16 [5632, 2048], P('head'), may hold values from -0.109375 to 0.109375
- out_grad: bfloat16 [2, 8192, 2048], P(None, 'seq', 'head'), may hold values from -6 to 6
Outputs:
- output: bfloat16 [2, 8192, 2048], P(None, 'seq', 'head')
- tokens_grad: bfloat16 [2, 8192, 2048], P(None, 'seq', 'head')
- norm_gain_grad: float32 [2048], P(('head', 'seq'))
- query_key_value_gradient: float32 [3, 2048, 2048], P(None, 'seq', 'head')
- strength_weight_gradient: float32 [2048, 16], P('seq', 'head')
- conv_grad: float32 [3, 4, 2048], P(None, None, ('head', 'seq'))
- head_gain_grad: float32 [128], P('seq')
- out_weight_grad: float32 [2048, 2048], P('head', 'seq')
- mlp_gain_grad: float32 [2048], P(('head', 'seq'))
- gate_up_grad: float32 [2, 2048, 5632], P(None, 'seq', 'head')
- down_projection_gradient: float32 [5632, 2048], P('head', 'seq')
Inputs may be any that keep to these rules, and one draw needn't show every extreme that they name: Sequence s has lengths[s] real tokens at the start of its 8192 positions and padding after them; one sequence, drawn from the seed, has exactly 8192.
All inputs are finite; a program needn't handle non-finite values.
Results may differ from a plain program's by a relative error of at most 0.04.
Values may be sent and summed in bfloat16 or wider, within the bound.
No kernel may reach another device: no remote copies, remote signals or barrier semaphores. Data moves between devices by JAX's collectives and lax.ppermute only.
A program may use at most 256 MiB of HBM per device.

v0:
```python
from functools import partial

import jax
import jax.numpy as jnp
from jax import lax
from jax.sharding import PartitionSpec as P

HEAD_DIM = 128
CONV = 4
BLOCK = 64


norm_eps = 1e-06
highest_precision = lax.Precision.HIGHEST


def from_behind(value, axis, steps):
    count = lax.axis_size(axis)
    initial, last = (max(0, -steps), min(count, count - steps))
    return lax.ppermute(value, axis, [(source, source + steps) for source in range(initial, last)])


def carried_in(part, axis, combine, identity):
    place = lax.axis_index(axis)
    gathered = jax.tree.map(lambda a: lax.all_gather(a, axis), part)
    state = jax.tree.map(lambda a, e: jnp.zeros_like(a) + jnp.asarray(e, a.dtype), part, identity)

    def one(hop, state):
        return combine(
            state, jax.tree.map(lambda a: lax.dynamic_index_in_dim(a, hop, 0, False), gathered)
        )

    return lax.fori_loop(0, place, one, state)


def entering(x, axis, combine, identity):
    size, mine = (lax.axis_size(axis), lax.axis_index(axis))
    everything = jax.tree.map(
        lambda part, kind: lax.all_gather(part.astype(kind), axis),
        x,
        jax.tree.map(lambda a: jnp.bfloat16 if a.dtype == jnp.float32 else a.dtype, x),
    )
    start = jax.tree.map(
        lambda part, zero: jnp.broadcast_to(jnp.asarray(zero, part.dtype), part.shape), x, identity
    )

    def hop(k, before):
        at = size - 1 - k
        reached = at > mine
        new = combine(
            before, jax.tree.map(lambda part, own: part[at].astype(own.dtype), everything, x)
        )
        return jax.tree.map(lambda a, b: jnp.where(reached, a, b), new, before)

    return lax.fori_loop(0, size, hop, start)


def row_norm(values, gain_vec):
    return (
        values * lax.rsqrt(jnp.mean(values * values, axis=-1, keepdims=True) + norm_eps) * gain_vec
    )


def unit_rows(values):
    return values * lax.rsqrt(jnp.sum(values * values, axis=-1, keepdims=True) + norm_eps)


def prepare(extended, logit_values, conv_weight, valid_mask):
    seq_count, length, heads_dev = logit_values.shape
    conv_mixed = conv_weight[:, 0][:, None, None, :] * extended[:, :, 0:length, :]
    for tap_index in range(1, CONV):
        conv_mixed = (
            conv_mixed
            + conv_weight[:, tap_index][:, None, None, :]
            * extended[:, :, tap_index : tap_index + length, :]
        )
    active = jax.nn.silu(conv_mixed)

    def by_head(tensor):
        grouped = tensor.reshape(seq_count, length, heads_dev, HEAD_DIM)
        return jnp.transpose(grouped, (0, 2, 1, 3)).reshape(seq_count * heads_dev, length, HEAD_DIM)

    queries = unit_rows(by_head(active[0]))
    keys_unit = unit_rows(by_head(active[1]))
    values = by_head(active[2])
    strength = jnp.transpose(
        jax.nn.sigmoid(logit_values) * valid_mask[:, :, None], (0, 2, 1)
    ).reshape(seq_count * heads_dev, length)
    return (queries, keys_unit, values, strength)


def span_free_pass(queries, keys_unit, values, strength):
    row_count, length, head_width = queries.shape
    num_blocks = length // BLOCK

    def blocked(tensor):
        shaped = tensor.reshape((row_count, num_blocks, BLOCK) + tensor.shape[2:])
        return jnp.swapaxes(shaped, 0, 1)

    eye_block = jnp.eye(BLOCK, dtype=jnp.float32)
    eye_state = jnp.eye(head_width, dtype=jnp.float32)

    def one_block(carried_pair, block_items):
        sofar_map, sofar_add = carried_pair
        query_blk, key_blk, value_blk, rate_blk = block_items
        key_inner = jnp.einsum("bik,bjk->bij", key_blk, key_blk, precision=highest_precision)
        system = eye_block + rate_blk[:, :, None] * jnp.tril(key_inner, -1)
        right_side = rate_blk[:, :, None] * jnp.concatenate([key_blk, value_blk], axis=2)
        solved = lax.linalg.triangular_solve(system, right_side, left_side=True, lower=True)
        weight_key = solved[:, :, :head_width]
        weight_value = solved[:, :, head_width:]
        scores = jnp.tril(
            jnp.einsum("bik,bjk->bij", query_blk, key_blk, precision=highest_precision)
        )
        reduced = query_blk - jnp.einsum(
            "bij,bjk->bik", scores, weight_key, precision=highest_precision
        )
        zero_part = jnp.einsum(
            "bik,bkv->biv", reduced, sofar_add, precision=highest_precision
        ) + jnp.einsum("bij,bjv->biv", scores, weight_value, precision=highest_precision)
        state_part = jnp.einsum("bik,bkm->bim", reduced, sofar_map, precision=highest_precision)
        step_map = eye_state - jnp.einsum(
            "bjk,bjm->bkm", key_blk, weight_key, precision=highest_precision
        )
        next_map = jnp.einsum("bkm,bmn->bkn", step_map, sofar_map, precision=highest_precision)
        next_add = jnp.einsum(
            "bkm,bmv->bkv", step_map, sofar_add, precision=highest_precision
        ) + jnp.einsum("bjk,bjv->bkv", key_blk, weight_value, precision=highest_precision)
        return ((next_map, next_add), (zero_part, state_part))

    initial = (
        jnp.broadcast_to(eye_state, (row_count, head_width, head_width)),
        jnp.zeros((row_count, head_width, head_width), jnp.float32),
    )
    (total_map, total_add), (zero_out, state_rows) = lax.scan(
        one_block,
        initial,
        (blocked(queries), blocked(keys_unit), blocked(values), blocked(strength)),
    )

    def unblocked(tensor):
        return jnp.swapaxes(tensor, 0, 1).reshape(row_count, length, head_width)

    return (total_map, total_add, unblocked(zero_out), unblocked(state_rows))


def finish(mixer, head_gain, valid_mask):
    seq_count, length = valid_mask.shape
    heads_dev = mixer.shape[0] // seq_count
    grouped = jnp.transpose(mixer.reshape(seq_count, heads_dev, length, HEAD_DIM), (0, 2, 1, 3))
    normed = row_norm(grouped, head_gain) * valid_mask[:, :, None, None]
    return normed.reshape(seq_count, length, heads_dev * HEAD_DIM)


def compose(first_part, second_part):
    map_first, add_first = first_part
    map_second, add_second = second_part
    joined_map = jnp.einsum("bij,bjk->bik", map_second, map_first, precision=highest_precision)
    joined_add = (
        jnp.einsum("bij,bjk->bik", map_second, add_first, precision=highest_precision) + add_second
    )
    return (joined_map, joined_add)


def mixer_local(extended, logit_values, conv_weight, head_gain, incoming, valid_mask):
    queries, keys_unit, values, strength = prepare(extended, logit_values, conv_weight, valid_mask)
    total_map, total_add, zero_out, state_rows = span_free_pass(
        queries, keys_unit, values, strength
    )
    mixer = zero_out + jnp.einsum("blk,bkv->blv", state_rows, incoming, precision=highest_precision)
    leaving = (
        jnp.einsum("bij,bjk->bik", total_map, incoming, precision=highest_precision) + total_add
    )
    return (finish(mixer, head_gain, valid_mask), leaving)


def norm_back(full_in, full_grad, gain_vec, col_start, width_dev):
    inv_rms = lax.rsqrt(jnp.mean(full_in * full_in, axis=-1, keepdims=True) + norm_eps)
    row_dot = jnp.mean(gain_vec * full_grad * full_in, axis=-1, keepdims=True)
    own_in = lax.dynamic_slice_in_dim(full_in, col_start, width_dev, 2)
    own_grad = lax.dynamic_slice_in_dim(full_grad, col_start, width_dev, 2)
    own_gain = lax.dynamic_slice_in_dim(gain_vec, col_start, width_dev, 0)
    input_grad = inv_rms * own_gain * own_grad - inv_rms * inv_rms * inv_rms * own_in * row_dot
    gain_grad = jnp.sum(own_grad * own_in * inv_rms, axis=(0, 1))
    return (input_grad, gain_grad)


def shards(
    tokens,
    lengths,
    norm_gain,
    query_key_value_weight,
    strength_projection,
    conv_weight,
    head_gain,
    output_projection,
    mlp_gain,
    gate_up_weight,
    down_projection,
    out_grad,
):
    seq_count, block_len, width_dev = tokens.shape
    col_start = lax.axis_index("head") * width_dev
    positions = lax.axis_index("seq") * block_len + jnp.arange(block_len, dtype=jnp.int32)
    valid_mask = (positions[None, :] < lengths[:, None]).astype(jnp.float32)
    full_rows = lax.all_gather(tokens, "head", axis=2, tiled=True).astype(jnp.float32)
    normalized_input = row_norm(full_rows, norm_gain).astype(jnp.bfloat16)
    projected_tokens = jnp.einsum(
        "pit,ftw->fpiw",
        normalized_input,
        query_key_value_weight,
        preferred_element_type=jnp.float32,
    ).astype(jnp.bfloat16)
    logit_values = jnp.einsum(
        "qbx,xg->qbg", normalized_input, strength_projection, preferred_element_type=jnp.float32
    )
    tail_rows = projected_tokens[:, :, block_len - (CONV - 1) :, :]
    before = from_behind(tail_rows, "seq", 1)
    extended = jnp.concatenate([before, projected_tokens], axis=2).astype(jnp.float32)
    queries, keys_unit, values, strength = prepare(extended, logit_values, conv_weight, valid_mask)
    total_map, total_add, zero_out, state_rows = span_free_pass(
        queries, keys_unit, values, strength
    )
    identity = (
        jnp.broadcast_to(jnp.eye(HEAD_DIM, dtype=jnp.float32), total_map.shape),
        jnp.zeros_like(total_add),
    )
    _, incoming = carried_in((total_map, total_add), "seq", compose, identity)
    mixer = zero_out + jnp.einsum("blk,bkv->blv", state_rows, incoming, precision=highest_precision)
    head_output = finish(mixer, head_gain, valid_mask).astype(jnp.bfloat16)
    attention_portion = jnp.einsum(
        "rpj,jk->rpk", head_output, output_projection, preferred_element_type=jnp.float32
    )
    middle_rows = full_rows + lax.psum(attention_portion, "head")
    middle_own = lax.dynamic_slice_in_dim(middle_rows, col_start, width_dev, 2)
    normalized_middle = row_norm(middle_rows, mlp_gain).astype(jnp.bfloat16)
    gated_preactivation = jnp.einsum(
        "rux,gxt->grut", normalized_middle, gate_up_weight, preferred_element_type=jnp.float32
    )
    hidden_features = (jax.nn.silu(gated_preactivation[0]) * gated_preactivation[1]).astype(
        jnp.bfloat16
    )
    feedforward_portion = jnp.einsum(
        "yqj,jo->yqo", hidden_features, down_projection, preferred_element_type=jnp.float32
    )
    mlp_own = lax.psum_scatter(
        feedforward_portion.astype(jnp.bfloat16), "head", scatter_dimension=2, tiled=True
    ).astype(jnp.float32)
    output = (middle_own + mlp_own).astype(jnp.bfloat16)
    gradient_rows = lax.all_gather(out_grad, "head", axis=2, tiled=True)
    down_projection_gradient = jnp.einsum(
        "rtq,rtx->qx", hidden_features, gradient_rows, preferred_element_type=jnp.float32
    )
    hidden_grad = jnp.einsum(
        "zxp,hp->zxh", gradient_rows, down_projection, preferred_element_type=jnp.float32
    )
    gate_sigmoid = jax.nn.sigmoid(gated_preactivation[0])
    gate_grad = (
        hidden_grad
        * gated_preactivation[1]
        * gate_sigmoid
        * (1.0 + gated_preactivation[0] * (1.0 - gate_sigmoid))
    )
    up_grad = hidden_grad * gated_preactivation[0] * gate_sigmoid
    gated_hidden_gradient = jnp.stack([gate_grad, up_grad]).astype(jnp.bfloat16)
    gate_up_grad = jnp.einsum(
        "qig,kqiv->kgv",
        normalized_middle,
        gated_hidden_gradient,
        preferred_element_type=jnp.float32,
    )
    mid_partial = jnp.einsum(
        "nyqp,ngp->yqg", gated_hidden_gradient, gate_up_weight, preferred_element_type=jnp.float32
    )
    mid_total = lax.psum(mid_partial.astype(jnp.bfloat16), "head").astype(jnp.float32)
    middle_back, mlp_gain_grad = norm_back(middle_rows, mid_total, mlp_gain, col_start, width_dev)
    middle_grad = out_grad.astype(jnp.float32) + middle_back
    branch_grad = middle_grad.astype(jnp.bfloat16)
    branch_token_rows = lax.all_gather(branch_grad, "head", axis=2, tiled=True)
    out_weight_grad = jnp.einsum(
        "gmx,gmv->xv", head_output, branch_token_rows, preferred_element_type=jnp.float32
    )
    head_grad = jnp.einsum(
        "hpj,wj->hpw", branch_token_rows, output_projection, preferred_element_type=jnp.float32
    )
    local_mixer = partial(mixer_local, valid_mask=valid_mask)
    _, pullback = jax.vjp(local_mixer, extended, logit_values, conv_weight, head_gain, incoming)
    zero_state = jnp.zeros_like(incoming)
    from_outputs = pullback((head_grad, zero_state))[4]
    _, leaving_grad = entering(
        (jnp.swapaxes(total_map, 1, 2), from_outputs), "seq", compose, identity
    )
    ext_grad, logit_grad, conv_grad, head_gain_grad, _ = pullback((head_grad, leaving_grad))
    sent_back = from_behind(ext_grad[:, :, : CONV - 1, :].astype(jnp.bfloat16), "seq", -1).astype(
        jnp.float32
    )
    projection_gradient = ext_grad[:, :, CONV - 1 :, :]
    projection_gradient = (
        projection_gradient.at[:, :, block_len - (CONV - 1) :, :]
        .add(sent_back)
        .astype(jnp.bfloat16)
    )
    logit_reduced_precision = logit_grad.astype(jnp.bfloat16)
    query_key_value_gradient = jnp.einsum(
        "kub,hkuy->hby", normalized_input, projection_gradient, preferred_element_type=jnp.float32
    )
    strength_weight_gradient = jnp.einsum(
        "qrg,qre->ge", normalized_input, logit_reduced_precision, preferred_element_type=jnp.float32
    )
    in_partial = jnp.einsum(
        "qxtm,qbm->xtb",
        projection_gradient,
        query_key_value_weight,
        preferred_element_type=jnp.float32,
    ) + jnp.einsum(
        "xzi,pi->xzp",
        logit_reduced_precision,
        strength_projection,
        preferred_element_type=jnp.float32,
    )
    in_total, head_gain_total = (
        lax.psum(in_partial.astype(jnp.bfloat16), "head").astype(jnp.float32),
        lax.psum(head_gain_grad.astype(jnp.bfloat16), "head").astype(jnp.float32),
    )
    tokens_back, norm_gain_grad = norm_back(full_rows, in_total, norm_gain, col_start, width_dev)
    tokens_grad = (tokens_back + middle_grad).astype(jnp.bfloat16)
    qkv_sum, beta_sum, conv_sum, out_sum, head_sum, norm_sum, gate_up_sum, down_sum, mlp_sum = (
        lax.psum_scatter(
            query_key_value_gradient.astype(jnp.bfloat16), "seq", scatter_dimension=1, tiled=True
        ).astype(jnp.float32),
        lax.psum_scatter(
            strength_weight_gradient.astype(jnp.bfloat16), "seq", scatter_dimension=0, tiled=True
        ).astype(jnp.float32),
        lax.psum_scatter(
            conv_grad.astype(jnp.bfloat16), "seq", scatter_dimension=2, tiled=True
        ).astype(jnp.float32),
        lax.psum_scatter(
            out_weight_grad.astype(jnp.bfloat16), "seq", scatter_dimension=1, tiled=True
        ).astype(jnp.float32),
        lax.psum_scatter(
            head_gain_total.astype(jnp.bfloat16), "seq", scatter_dimension=0, tiled=True
        ).astype(jnp.float32),
        lax.psum_scatter(
            norm_gain_grad.astype(jnp.bfloat16), "seq", scatter_dimension=0, tiled=True
        ).astype(jnp.float32),
        lax.psum_scatter(
            gate_up_grad.astype(jnp.bfloat16), "seq", scatter_dimension=1, tiled=True
        ).astype(jnp.float32),
        lax.psum_scatter(
            down_projection_gradient.astype(jnp.bfloat16), "seq", scatter_dimension=1, tiled=True
        ).astype(jnp.float32),
        lax.psum_scatter(
            mlp_gain_grad.astype(jnp.bfloat16), "seq", scatter_dimension=0, tiled=True
        ).astype(jnp.float32),
    )
    return (
        output,
        tokens_grad,
        norm_sum,
        qkv_sum,
        beta_sum,
        conv_sum,
        head_sum,
        out_sum,
        mlp_sum,
        gate_up_sum,
        down_sum,
    )


def solution(mesh):
    return jax.shard_map(
        shards,
        mesh=mesh,
        in_specs=(
            P(None, "seq", "head"),
            P(),
            P(),
            P(None, None, "head"),
            P(None, "head"),
            P(None, None, "head"),
            P(),
            P("head", None),
            P(),
            P(None, None, "head"),
            P("head", None),
            P(None, "seq", "head"),
        ),
        out_specs=(
            P(None, "seq", "head"),
            P(None, "seq", "head"),
            P(("head", "seq")),
            P(None, "seq", "head"),
            P("seq", "head"),
            P(None, None, ("head", "seq")),
            P("seq"),
            P("head", "seq"),
            P(("head", "seq")),
            P(None, "seq", "head"),
            P("head", "seq"),
        ),
        check_vma=False,
    )
```

profile of v0, /device:TPU:2, one launch (start us, length us, event | category | flops | bytes accessed | tf_op | source)
XLA Modules:
  0.0 1919.1 jit_solution(18252076833871366321)
XLA Ops:
  9.7 32.2 %all-gather.12.cloned.1.call-done = bf16[2,256,2048]{2,1,0:T(8,128)(2,1)} async-done(((bf16[2,256,512]{2,1,0:T(8,128)(2,1)}), bf16[2,256,2048]{2,1,0:T(8,128)(2,1)}) %all-gather.12.cloned.1.call-update) | async-done | bytes 2097168 | tf_op jit(solution)/shard_map/all_gather | solution.py:206
  44.6 7.0 fusion.238
  56.9 3.2 fusion.220
  64.9 2.5 reshape_squeeze.9
  81.4 215.0 %while.121 = (s32[]{:T(128)}, f32[8,128,128]{2,1,0:T(8,128)}, f32[8,128,128]{2,1,0:T(8,128)}, f32[4,8,64,128]{3,2,0,1:T(8,128)}, f32[4,8,64,128]{3,2,0,1:T(8,128...) while((s32[]{:T(128)}, f32[8,128,128]{2,1,0:T(8,128)}, ...), condition=%wide.region_4.6_spmd.clone, body=%wide.region_3.5_spmd.clone.sunk | while | flops 1108426752 | bytes 17627296 | solution.py:135
  83.2 39.3 %custom-call.41 = f32[8,1,64,64]{2,3,1,0:T(8,128)S(1)} custom-call(f32[8,1,64,64]{3,2,1,0:T(8,128)S(1)} %fusion.544), custom_call_target="InvertDiagBlocksLowerTriangular" | custom-call | tf_op jit(solution)/shard_map/while/body/eval_jaxpr/triangular_solve/custom-call.1 | solution.py:109
  136.9 39.3 %custom-call.41 = f32[8,1,64,64]{2,3,1,0:T(8,128)S(1)} custom-call(f32[8,1,64,64]{3,2,1,0:T(8,128)S(1)} %fusion.544), custom_call_target="InvertDiagBlocksLowerTriangular" | custom-call | tf_op jit(solution)/shard_map/while/body/eval_jaxpr/triangular_solve/custom-call.1 | solution.py:109
  190.7 39.3 %custom-call.41 = f32[8,1,64,64]{2,3,1,0:T(8,128)S(1)} custom-call(f32[8,1,64,64]{3,2,1,0:T(8,128)S(1)} %fusion.544), custom_call_target="InvertDiagBlocksLowerTriangular" | custom-call | tf_op jit(solution)/shard_map/while/body/eval_jaxpr/triangular_solve/custom-call.1 | solution.py:109
  244.4 39.3 %custom-call.41 = f32[8,1,64,64]{2,3,1,0:T(8,128)S(1)} custom-call(f32[8,1,64,64]{3,2,1,0:T(8,128)S(1)} %fusion.544), custom_call_target="InvertDiagBlocksLowerTriangular" | custom-call | tf_op jit(solution)/shard_map/while/body/eval_jaxpr/triangular_solve/custom-call.1 | solution.py:109
  297.4 2.5 copy.172
  300.0 72.1 %all-gather.18.cloned.1.call-done = f32[256,128,128]{2,1,0:T(8,128)} async-done(((f32[8,128,128]{2,1,0:T(8,128)}), f32[256,128,128]{2,1,0:T(8,128)}) %all-gather.18.cloned.1.call-update) | async-done | bytes 16777232 | tf_op jit(solution)/shard_map/all_gather | solution.py:25
  372.1 74.9 %all-gather.20.cloned.1.call-done = f32[256,128,128]{2,1,0:T(8,128)} async-done(((f32[8,128,128]{2,1,0:T(8,128)}), f32[256,128,128]{2,1,0:T(8,128)}) %all-gather.20.cloned.1.call-update) | async-done | bytes 16777232 | tf_op jit(solution)/shard_map/all_gather | solution.py:25
  447.0 2.8 convolution_add_fusion.19
  451.0 3.3 fusion.231
  454.9 149.4 %all-reduce.25.cloned.1.call-done = f32[2,256,2048]{2,1,0:T(8,128)} async-done(((f32[2,256,2048]{2,1,0:T(8,128)}), f32[2,256,2048]{2,1,0:T(8,128)}) %all-reduce.25.cloned.1.call-update) | async-done | bytes 4194320 | tf_op jit(solution)/shard_map/psum | solution.py:234
  604.3 3.5 multiply_reduce_fusion.2
  609.8 11.3 fusion.210
  621.1 15.7 all-gather.14.cloned.1.call-done
  636.8 10.4 fusion.244
  648.8 10.1 bitcast_convert_fusion.4
  659.0 58.5 %all-reduce.27.cloned.1.call-done = bf16[2,256,2048]{2,1,0:T(8,128)(2,1)} async-done(((bf16[2,256,2048]{2,1,0:T(8,128)(2,1)}), bf16[2,256,2048]{2,1,0:T(8,128)(2,1)}) %all-reduce.27.cloned.1.call-update) | async-done | bytes 2097168 | tf_op jit(solution)/shard_map/psum | solution.py:275
  717.5 3.6 multiply_reduce_fusion.1
  729.7 248.3 %while.122 = (s32[]{:T(128)}, f32[8,128,128]{2,1,0:T(8,128)}, f32[8,128,128]{2,1,0:T(8,128)}, f32[4,8,64,128]{3,2,1,0:T(8,128)}, f32[4,8,64,128]{3,2,0,1:T(8,128...) while((s32[]{:T(128)}, f32[8,128,128]{2,1,0:T(8,128)}, ...), condition=%wide.region_12.14_spmd.clone, body=%wide.region_11.13_spmd.clone.sunk | while | flops 1108750336 | bytes 26720072 | solution.py:135
  732.4 40.0 %custom-call.42 = f32[8,1,64,64]{2,3,1,0:T(8,128)} custom-call(f32[8,1,64,64]{3,2,1,0:T(8,128)S(1)} %select_bitcast_fusion.5), custom_call_target="InvertDiagBlocksLowerTriangular" | custom-call | tf_op jit(solution)/shard_map/jvp()/while/body/eval_jaxpr/triangular_solve/custom-call.1 | solution.py:109
  772.4 2.5 bitcast_dynamic-update-slice_fusion.20
  794.4 40.0 %custom-call.42 = f32[8,1,64,64]{2,3,1,0:T(8,128)} custom-call(f32[8,1,64,64]{3,2,1,0:T(8,128)S(1)} %select_bitcast_fusion.5), custom_call_target="InvertDiagBlocksLowerTriangular" | custom-call | tf_op jit(solution)/shard_map/jvp()/while/body/eval_jaxpr/triangular_solve/custom-call.1 | solution.py:109
  856.4 40.0 %custom-call.42 = f32[8,1,64,64]{2,3,1,0:T(8,128)} custom-call(f32[8,1,64,64]{3,2,1,0:T(8,128)S(1)} %select_bitcast_fusion.5), custom_call_target="InvertDiagBlocksLowerTriangular" | custom-call | tf_op jit(solution)/shard_map/jvp()/while/body/eval_jaxpr/triangular_solve/custom-call.1 | solution.py:109
  918.4 40.0 %custom-call.42 = f32[8,1,64,64]{2,3,1,0:T(8,128)} custom-call(f32[8,1,64,64]{3,2,1,0:T(8,128)S(1)} %select_bitcast_fusion.5), custom_call_target="InvertDiagBlocksLowerTriangular" | custom-call | tf_op jit(solution)/shard_map/jvp()/while/body/eval_jaxpr/triangular_solve/custom-call.1 | solution.py:109
  958.4 2.5 bitcast_dynamic-update-slice_fusion.20
  983.6 2.6 copy.183
  987.5 3.0 fusion.229
  992.4 2.6 fusion.245
  995.1 4.2 bitcast_convert_fusion.3
  999.5 7.9 bitcast_convert_fusion.2
  1011.1 4.3 fusion.282
  1019.1 30.1 %all-gather.24.cloned.1.call-done = bf16[256,128,128]{2,1,0:T(8,128)(2,1)} async-done(((bf16[8,128,128]{2,1,0:T(8,128)(2,1)}), bf16[256,128,128]{2,1,0:T(8,128)(2,1)}) %all-gather.24.cloned.1.call-update) | async-done | bytes 8388624 | tf_op jit(solution)/shard_map/all_gather | solution.py:39
  1049.3 50.9 %while.123 = (s32[]{:T(128)}, f32[8,128,128]{2,1,0:T(8,128)S(1)}, s32[]{:T(128)}, bf16[32,8,128,128]{3,2,1,0:T(8,128)(2,1)}, bf16[32,8,128,128]{3,2,1,0:T(8,128)...) while((s32[]{:T(128)}, f32[8,128,128]{2,1,0:T(8,128)S(1)}, s32[]{:T(128)}, ...), condition=%wide.region_18.20_spmd.clone, body=%wide.region_17.19_spmd.clone.sunk | while | flops 201981952 | bytes 3148445 | solution.py:55
  1105.6 329.8 %while.120 = (s32[]{:T(128)}, f32[8,128,128]{2,1,0:T(8,128)}, f32[8,128,128]{2,1,0:T(8,128)S(1)}, f32[4,8,64,128]{3,2,0,1:T(8,128)}, f32[4,8,64,128]{3,2,0,1:T(8...) while((s32[]{:T(128)}, f32[8,128,128]{2,1,0:T(8,128)}, ...), condition=%wide.region_22.24_spmd.clone.clone, body=%wide.region_19.23_spmd.clone.clone.sunk | while | flops 2242022912 | bytes 58386924 | solution.py:135
  1121.6 40.7 %custom-call.40 = f32[8,1,64,64]{2,3,1,0:T(8,128)} custom-call(f32[8,1,64,64]{3,2,1,0:T(8,128)} %select_bitcast_fusion.4), custom_call_target="InvertDiagBlocksLowerTriangular" | custom-call | tf_op jit(solution)/shard_map/transpose(jvp())/while/body/eval_jaxpr/triangular_solve | solution.py:109
  1204.0 40.7 %custom-call.40 = f32[8,1,64,64]{2,3,1,0:T(8,128)} custom-call(f32[8,1,64,64]{3,2,1,0:T(8,128)} %select_bitcast_fusion.4), custom_call_target="InvertDiagBlocksLowerTriangular" | custom-call | tf_op jit(solution)/shard_map/transpose(jvp())/while/body/eval_jaxpr/triangular_solve | solution.py:109
  1286.3 40.7 %custom-call.40 = f32[8,1,64,64]{2,3,1,0:T(8,128)} custom-call(f32[8,1,64,64]{3,2,1,0:T(8,128)} %select_bitcast_fusion.4), custom_call_target="InvertDiagBlocksLowerTriangular" | custom-call | tf_op jit(solution)/shard_map/transpose(jvp())/while/body/eval_jaxpr/triangular_solve | solution.py:109
  1368.6 40.7 %custom-call.40 = f32[8,1,64,64]{2,3,1,0:T(8,128)} custom-call(f32[8,1,64,64]{3,2,1,0:T(8,128)} %select_bitcast_fusion.4), custom_call_target="InvertDiagBlocksLowerTriangular" | custom-call | tf_op jit(solution)/shard_map/transpose(jvp())/while/body/eval_jaxpr/triangular_solve | solution.py:109
  1444.3 2.8 reshape.457
  1447.1 2.9 copy.195
  1450.1 2.6 reshape.453
  1452.7 5.7 multiply_reduce_fusion.7
  1459.7 3.5 broadcast_multiply_fusion.1
  1468.1 2.7 fusion.264
  1471.6 3.5 slice.162
  1478.9 9.3 fusion.213
  1488.3 7.9 fusion.221
  1496.2 11.6 fusion.200
  1507.8 29.0 %copy.206 = bf16[2,2048,1408]{2,0,1:T(2,128)(2,1)} copy(bf16[2,2048,1408]{1,2,0:T(8,128)(2,1)} %fusion.200) | data formatting | bytes 23068672 | tf_op jit(solution)/shard_map/convert_element_type | solution.py:347
  1536.8 7.0 fusion.201
  1543.8 14.1 copy.202
  1561.1 2.5 convert_element_type.197
  1568.3 57.3 %reduce-scatter.16.cloned.1.call-done = bf16[64,4]{1,0:T(8,128)(2,1)} async-done(((bf16[2048,4]{1,0:T(8,128)(2,1)}), bf16[64,4]{1,0:T(8,128)(2,1)}) %reduce-scatter.16.cloned.1.call-update) | async-done | bytes 528
  1626.4 58.3 %all-reduce.29.cloned.1.call-done = bf16[2,256,2048]{2,1,0:T(8,128)(2,1)} async-done(((bf16[2,256,2048]{2,1,0:T(8,128)(2,1)}), bf16[2,256,2048]{2,1,0:T(8,128)(2,1)}) %all-reduce.29.cloned.1.call-update) | async-done | bytes 2097168 | tf_op jit(solution)/shard_map/psum | solution.py:322
  1684.7 4.2 convert_element_type.225
  1689.8 26.6 %reduce-scatter.10.cloned.1.call-done = bf16[2,256,512]{2,1,0:T(8,128)(2,1)} async-done(((bf16[2,256,2048]{2,1,0:T(8,128)(2,1)}), bf16[2,256,512]{2,1,0:T(8,128)(2,1)}) %reduce-scatter.10.cloned.1.call-update) | async-done | bytes 524304 | tf_op jit(solution)/shard_map/reduce_scatter | solution.py:246
  1716.4 3.7 multiply_reduce_fusion.8
  1720.1 68.4 %all-reduce.18 = (bf16[512]{0:T(512)(128)(2,1)S(1)}, bf16[128]{0:T(256)(128)(2,1)S(1)}, bf16[512]{0:T(512)(128)(2,1)S(1)}) all-reduce(bf16[512]{0:T(512)(128)(2,1)S(1)} %get-tuple-element.1891, bf16[128]{0:T(256)(128)(2,1)S(1)} %get-tuple-element.1716, ...), channel_id=7, replica_groups=mesh['seq'=32,'head'=4] {'seq'}, use_global_device_ids=true, to_apply=%region_28.30.clone | all-reduce | flops 1152 | bytes 4608
  1789.2 9.6 psum.32
  1800.5 107.8 %all-reduce.31.cloned.1.call-done = (bf16[3,2048,512]{2,0,1:T(4,128)(2,1)}, bf16[2,2048,1408]{2,0,1:T(2,128)(2,1)}) async-done(((bf16[3,2048,512]{2,0,1:T(4,128)(2,1)}, bf16[2,2048,1408]{2,0,1:T(2,128)(2,1)}), (bf16[3,2048,512]{2,0,1:T(4,128)(2,1)}, bf16[2,2048,1408]{2,0,1:T(2,128)(2,1)})) %all-reduce.31.cloned.1.call-update) | async-done | bytes 17825808
  (724 shorter events, 454.1 us)
Async XLA Ops:
  7.2 443.8 %copy-start = (bf16[512,2048]{1,0:T(8,128)(2,1)S(1)}, bf16[512,2048]{1,0:T(8,128)(2,1)}, u32[]{:S(2)}) copy-start(bf16[512,2048]{1,0:T(8,128)(2,1)} %param.33) | copy-start | bytes 6291460
  7.2 34.8 %all-gather.12.cloned.1.call-start = ((), (), s32[]{:S(2)}) async-start(), calls=%async_computation.5 | async-start | bytes 2621440 | tf_op jit(solution)/shard_map/all_gather | solution.py:206
  7.9 364.1 %all-gather.18.cloned.1.call-start = ((), (), s32[]{:S(2)}) async-start(), calls=%async_computation.14 | async-start | bytes 17301504 | tf_op jit(solution)/shard_map/all_gather | solution.py:25
  9.7 47.2 %copy-start.40 = (f32[3,512]{1,0:T(4,128)}, f32[3,512]{1,0:T(4,128)S(1)}, u32[]{:S(2)}) copy-start(f32[3,512]{1,0:T(4,128)S(1)} %get-tuple-element.1909) | copy-start | bytes 18436
  9.7 47.2 %copy-start.42 = (f32[3,512]{1,0:T(4,128)}, f32[3,512]{1,0:T(4,128)S(1)}, u32[]{:S(2)}) copy-start(f32[3,512]{1,0:T(4,128)S(1)} %get-tuple-element.1910) | copy-start | bytes 18436
  9.7 47.2 %copy-start.44 = (f32[3,512]{1,0:T(4,128)}, f32[3,512]{1,0:T(4,128)S(1)}, u32[]{:S(2)}) copy-start(f32[3,512]{1,0:T(4,128)S(1)} %get-tuple-element.1911) | copy-start | bytes 18436
  9.7 47.2 %copy-start.46 = (f32[3,512]{1,0:T(4,128)}, f32[3,512]{1,0:T(4,128)S(1)}, u32[]{:S(2)}) copy-start(f32[3,512]{1,0:T(4,128)S(1)} %get-tuple-element.1912) | copy-start | bytes 18436
  44.6 8.8 copy-start.71
  44.6 8.8 copy-start.11
  44.6 8.8 copy-start.64
  44.6 8.9 copy-start.67
  51.7 3.2 collective-permute-start
  63.8 7.5 copy-start.48
  296.4 150.5 %all-gather.20.cloned.1.call-start = ((), (), s32[]{:S(2)}) async-start(), calls=%async_computation.15 | async-start | bytes 17301504 | tf_op jit(solution)/shard_map/all_gather | solution.py:25
  297.2 307.2 %all-reduce.25.cloned.1.call-start = ((), (), s32[]{:S(2)}) async-start(), calls=%async_computation.6 | async-start | bytes 8388608 | tf_op jit(solution)/shard_map/psum | solution.py:234
  454.3 182.5 %all-gather.14.cloned.1.call-start = ((), (), s32[]{:S(2)}) async-start(), calls=%async_computation.8 | async-start | bytes 2621440 | tf_op jit(solution)/shard_map/all_gather | solution.py:250
  454.9 154.9 %copy-start.66 = (f32[2048]{0:T(1024)S(1)}, f32[2048]{0:T(1024)}, u32[]{:S(2)}) copy-start(f32[2048]{0:T(1024)} %param.34) | copy-start | bytes 24580
  454.9 262.6 %all-reduce.27.cloned.1.call-start = ((), (), s32[]{:S(2)}) async-start(), calls=%async_computation.9 | async-start | bytes 4194304 | tf_op jit(solution)/shard_map/psum | solution.py:275
  607.8 113.9 %copy-start.58 = (f32[2,256]{1,0:T(2,128)}, f32[2,256]{1,0:T(2,128)S(1)}, u32[]{:S(2)}) copy-start(f32[2,256]{1,0:T(2,128)S(1)} %get-tuple-element.1907) | copy-start | bytes 6148
  658.9 328.6 %all-gather.16.cloned.1.call-start = ((), (), s32[]{:S(2)}) async-start(), calls=%async_computation.10 | async-start | bytes 2621440 | tf_op jit(solution)/shard_map/all_gather | solution.py:279
  659.0 62.7 %copy-start.60 = (f32[512]{0:T(512)}, f32[512]{0:T(512)S(1)}, u32[]{:S(2)}) copy-start(f32[512]{0:T(512)S(1)} %dynamic_slice.276) | copy-start | bytes 6148
  726.1 293.0 %all-gather.22.cloned.1.call-start = ((), (), s32[]{:S(2)}) async-start(), calls=%async_computation.16 | async-start | bytes 8650752 | tf_op jit(solution)/shard_map/all_gather | solution.py:39
  727.3 322.0 %all-gather.24.cloned.1.call-start = ((), (), s32[]{:S(2)}) async-start(), calls=%async_computation.17 | async-start | bytes 8650752 | tf_op jit(solution)/shard_map/all_gather | solution.py:39
  730.8 44.1 %copy-start.4 = (f32[8,64,128]{2,1,0:T(8,128)}, f32[8,64,128]{2,1,0:T(8,128)S(1)}, u32[]{:S(2)}) copy-start(f32[8,64,128]{2,1,0:T(8,128)S(1)} %get-tuple-element.2352) | copy-start | bytes 786436 | tf_op jit(solution)/shard_map/jvp()/while
  792.8 44.0 %copy-start.4 = (f32[8,64,128]{2,1,0:T(8,128)}, f32[8,64,128]{2,1,0:T(8,128)S(1)}, u32[]{:S(2)}) copy-start(f32[8,64,128]{2,1,0:T(8,128)S(1)} %get-tuple-element.2352) | copy-start | bytes 786436 | tf_op jit(solution)/shard_map/jvp()/while
  854.8 44.0 %copy-start.4 = (f32[8,64,128]{2,1,0:T(8,128)}, f32[8,64,128]{2,1,0:T(8,128)S(1)}, u32[]{:S(2)}) copy-start(f32[8,64,128]{2,1,0:T(8,128)S(1)} %get-tuple-element.2352) | copy-start | bytes 786436 | tf_op jit(solution)/shard_map/jvp()/while
  916.9 44.0 %copy-start.4 = (f32[8,64,128]{2,1,0:T(8,128)}, f32[8,64,128]{2,1,0:T(8,128)S(1)}, u32[]{:S(2)}) copy-start(f32[8,64,128]{2,1,0:T(8,128)S(1)} %get-tuple-element.2352) | copy-start | bytes 786436 | tf_op jit(solution)/shard_map/jvp()/while
  995.1 568.5 %reduce-scatter.12.cloned.1.call-start = ((), (), s32[]{:S(2)}) async-start(), calls=%async_computation.12 | async-start | bytes 2162688 | tf_op jit(solution)/shard_map/reduce_scatter | solution.py:337
  999.4 565.7 %reduce-scatter.14.cloned.1.call-start = ((), (), s32[]{:S(2)}) async-start(), calls=%async_computation.13 | async-start | bytes 5947392 | tf_op jit(solution)/shard_map/reduce_scatter | solution.py:349
  1007.4 559.4 %reduce-scatter.18.cloned.1.call-start = ((), (), s32[]{:S(2)}) async-start(), calls=%async_computation.19 | async-start | bytes 135168
  1105.6 331.7 %copy-start.53 = (f32[2,4,256]{2,1,0:T(4,128)S(1)}, f32[2,4,256]{2,1,0:T(4,128)}, u32[]{:S(2)}) copy-start(f32[2,4,256]{2,1,0:T(4,128)} %copy-done.52) | copy-start | bytes 24580
  1105.6 331.7 %copy-start.55 = (f32[2,4,256]{2,1,0:T(4,128)S(1)}, f32[2,4,256]{2,1,0:T(4,128)}, u32[]{:S(2)}) copy-start(f32[2,4,256]{2,1,0:T(4,128)} %copy-done.54) | copy-start | bytes 24580
  1106.0 8.9 copy-start.8
  1108.4 8.7 copy-start.32
  1166.2 8.0 copy-start.18
  1172.5 10.0 copy-start.31
  1174.2 9.3 copy-start.22
  1188.4 9.0 copy-start.8
  1190.8 8.7 copy-start.32
  1248.6 8.0 copy-start.18
  1254.8 10.0 copy-start.31
  1256.5 9.3 copy-start.22
  1270.7 8.9 copy-start.8
  1273.1 8.7 copy-start.32
  1330.9 8.0 copy-start.18
  1337.0 10.1 copy-start.31
  1338.8 9.3 copy-start.22
  1353.0 8.9 copy-start.8
  1355.4 8.7 copy-start.32
  1413.1 8.0 copy-start.18
  1419.3 10.1 copy-start.31
  1421.1 9.3 copy-start.22
  1444.3 8.3 copy-start.3
  1466.6 9.7 collective-permute-start.1
  1470.9 154.7 %reduce-scatter.16.cloned.1.call-start = ((), (), s32[]{:S(2)}) async-start(), calls=%async_computation.18 | async-start | bytes 540672
  1476.2 208.5 %all-reduce.29.cloned.1.call-start = ((), (), s32[]{:S(2)}) async-start(), calls=%async_computation.11 | async-start | bytes 4194304 | tf_op jit(solution)/shard_map/psum | solution.py:322
  1488.2 228.1 %reduce-scatter.10.cloned.1.call-start = ((), (), s32[]{:S(2)}) async-start(), calls=%async_computation.7 | async-start | bytes 2621440 | tf_op jit(solution)/shard_map/reduce_scatter | solution.py:246
  1496.1 412.2 %all-reduce.31.cloned.1.call-start = ((), (), s32[]{:S(2)}) async-start(), calls=%async_computation.20 | async-start | bytes 39845888
  1688.9 27.4 %copy-start.34 = (bf16[2,256,512]{2,1,0:T(8,128)(2,1)S(1)}, bf16[2,256,512]{2,1,0:T(8,128)(2,1)}, u32[]{:S(2)}) copy-start(bf16[2,256,512]{2,1,0:T(8,128)(2,1)} %param.37) | copy-start | bytes 1572868
  1688.9 27.4 %copy-start.59 = (f32[2,256]{1,0:T(2,128)S(1)}, f32[2,256]{1,0:T(2,128)}, u32[]{:S(2)}) copy-start(f32[2,256]{1,0:T(2,128)} %copy-done.58) | copy-start | bytes 6148
  1688.9 27.4 %copy-start.61 = (f32[512]{0:T(512)S(1)}, f32[512]{0:T(512)}, u32[]{:S(2)}) copy-start(f32[512]{0:T(512)} %copy-done.60) | copy-start | bytes 6148
  1688.9 27.4 %copy-start.63 = (f32[2,256]{1,0:T(2,128)S(1)}, f32[2,256]{1,0:T(2,128)}, u32[]{:S(2)}) copy-start(f32[2,256]{1,0:T(2,128)} %copy-done.62) | copy-start | bytes 6148
  1689.0 27.4 %copy-start.70 = (f32[2,256]{1,0:T(2,128)S(1)}, f32[2,256]{1,0:T(2,128)}, u32[]{:S(2)}) copy-start(f32[2,256]{1,0:T(2,128)} %get-tuple-element.1905) | copy-start | bytes 6148
  1716.4 195.9 %copy-start.1 = (bf16[512,2048]{1,0:T(8,128)(2,1)S(1)}, bf16[512,2048]{1,0:T(8,128)(2,1)}, u32[]{:S(2)}) copy-start(bf16[512,2048]{1,0:T(8,128)(2,1)} %param.33) | copy-start | bytes 6291460
  (60 other events, 224.0 us)
Sparse Core Ops, SparseCore 0:
  9.7 32.2 all-gather.11
  296.5 75.4 all-gather.17
  374.9 71.9 all-gather.19
  454.4 149.8 all-reduce.24
  605.9 30.8 all-gather.13
  659.0 58.4 all-reduce.26
  726.3 31.4 all-gather.15
  760.5 54.1 all-gather.21
  995.2 54.0 all-gather.23
  1052.6 78.6 reduce-scatter.11
  1135.0 85.2 reduce-scatter.13
  1471.0 73.7 reduce-scatter.17
  1549.2 76.3 reduce-scatter.15
  1627.9 56.7 all-reduce.28
  1686.9 29.3 reduce-scatter.9
  1720.7 187.5 all-reduce.30
where the time goes:
time: 1930 us; the launch traced here: 1920 us
  waiting for transfers between devices  685 us (35%)
  other arithmetic  559 us (29%)
  matrix products  428 us (22%)
  local copies, waits for them, and re-layouts  144 us (7%)
  blocking collectives  78 us (4%)
    another operation x32, other arithmetic, one_block(): lax.linalg.triangular_solve(system, right_side, left_side=True, lower=True)  488 us
    unnamed x19, waiting for transfers between devices  167 us
    psum x1, waiting for transfers between devices, shards(): middle_rows = full_rows + lax.psum(attention_portion, 'head')  149 us
    all_gather x2, waiting for transfers between devices, carried_in(): gathered = jax.tree.map(lambda a: lax.all_gather(a, axis), part)  147 us
    unnamed x1, blocking collectives  68.4 us
    psum x1, waiting for transfers between devices, shards(): lax.psum(mid_partial.astype(jnp.bfloat16), 'head').astype(jnp.float32)  58.5 us
    psum x1, waiting for transfers between devices, shards(): lax.psum(in_partial.astype(jnp.bfloat16), 'head').astype(jnp.float32)  58.3 us
    dot_general x32, matrix products, compose(): jnp.einsum('bij,bjk->bik', map_second, add_first, precision=highest_preci...  48.4 us
  transfers between devices with their start and end apart: 18, of which 11 were waited for; matrix products, arithmetic and copies ran while one was open for 43% of the time, Pallas kernels for 0%

commit v1 on v0

v1 whole, which is shorter than its diff:
```python
from functools import partial

import jax
import jax.numpy as jnp
from jax import lax
from jax.experimental import pallas as pl
from jax.experimental.pallas import tpu as pltpu
from jax.sharding import PartitionSpec as P

HEAD_DIM = 128
CONV = 4
HALF = 128
HALO = 8
EPS = 1e-06

f32 = jnp.float32
bf16 = jnp.bfloat16


def dot(a, b, dims=((1,), (0,))):
    return lax.dot_general(
        a.astype(bf16), b.astype(bf16), (dims, ((), ())), preferred_element_type=f32
    )


NT = ((1,), (1,))
TN = ((0,), (0,))


def split(a):
    high = a.astype(bf16)
    return high, (a - high.astype(f32)).astype(bf16)


def dot3(a, b):
    a_high, a_low = split(a)
    b_high, b_low = split(b)
    return dot(a_high, b_high) + (dot(a_high, b_low) + dot(a_low, b_high))


def unit_lower_inverse(strict):
    size = strict.shape[0]
    row = lax.broadcasted_iota(jnp.int32, (size, size), 0)
    col = lax.broadcasted_iota(jnp.int32, (size, size), 1)
    inverse = jnp.where(row == col, 1.0, 0.0)
    width = 1
    while width < size:
        below = (row // (2 * width) == col // (2 * width)) & (row // width != col // width)
        part = jnp.where(below, strict, 0.0)
        if width == 1:
            inverse = inverse - part
        else:
            inverse = inverse - dot3(inverse, dot3(part, inverse))
        width *= 2
    return inverse


def sigmoid(x):
    return 1.0 / (1.0 + jnp.exp(-x))


def masks():
    row = lax.broadcasted_iota(jnp.int32, (HALF, HALF), 0)
    col = lax.broadcasted_iota(jnp.int32, (HALF, HALF), 1)
    return row > col, row >= col


def conv_rows(j, proj_ref, halo_ref, conv_ref, rows, lanes):
    length = proj_ref.shape[2]
    rows[0:HALO, :] = halo_ref[j, 0, :, lanes].astype(f32)
    rows[HALO : HALO + length, :] = proj_ref[j, 0, :, lanes].astype(f32)
    mixed = None
    for i in range(CONV):
        start = HALO - (CONV - 1) + i
        term = conv_ref[j, i : i + 1, lanes] * rows[start : start + length, :]
        mixed = term if mixed is None else mixed + term
    return mixed


def column_of(values, at):
    lane = lax.broadcasted_iota(jnp.int32, values.shape, 1)
    return jnp.sum(jnp.where(lane == at, values, 0.0), axis=1, keepdims=True)


def span_kernel(
    heads, proj_ref, halo_ref, conv_ref, strength_ref,
    send_ref, q_ref, k_ref, v_ref, w_ref, u_ref, gram_ref, score_ref, inv_ref, rows,
):
    lower, lower_diag = masks()
    for h in range(heads):
        lanes = slice(h * HEAD_DIM, (h + 1) * HEAD_DIM)
        active = []
        for j in range(3):
            mixed = conv_rows(j, proj_ref, halo_ref, conv_ref, rows.at[h * 3 + j], lanes)
            active.append(mixed * sigmoid(mixed))
        q = active[0] * lax.rsqrt(jnp.sum(active[0] * active[0], axis=1, keepdims=True) + EPS)
        k = active[1] * lax.rsqrt(jnp.sum(active[1] * active[1], axis=1, keepdims=True) + EPS)
        v = active[2]
        q_ref[h] = q.astype(bf16)
        k_ref[h] = k.astype(bf16)
        v_ref[h] = v.astype(bf16)
        beta = column_of(strength_ref[0], h)
        gram = dot(k, k, NT)
        score = dot(q, k, NT)
        a, b = slice(0, HALF), slice(HALF, 2 * HALF)
        gaa = jnp.where(lower, gram[a, a], 0.0)
        gbb = jnp.where(lower, gram[b, b], 0.0)
        gba = gram[b, a]
        gram_ref[h, 0] = gaa.astype(bf16)
        gram_ref[h, 1] = gba.astype(bf16)
        gram_ref[h, 2] = gbb.astype(bf16)
        score_ref[h, 0] = jnp.where(lower_diag, score[a, a], 0.0).astype(bf16)
        score_ref[h, 1] = score[b, a].astype(bf16)
        score_ref[h, 2] = jnp.where(lower_diag, score[b, b], 0.0).astype(bf16)
        taa = unit_lower_inverse(beta[a] * gaa)
        tbb = unit_lower_inverse(beta[b] * gbb)
        inv_ref[h, 0] = taa.astype(bf16)
        inv_ref[h, 1] = tbb.astype(bf16)
        right = beta * jnp.concatenate([k, v], axis=1)
        top = dot(taa, right[a])
        bottom = dot(tbb, right[b] - beta[b] * dot(gba, top))
        w = jnp.concatenate([top[:, :HEAD_DIM], bottom[:, :HEAD_DIM]], axis=0)
        u = jnp.concatenate([top[:, HEAD_DIM:], bottom[:, HEAD_DIM:]], axis=0)
        w_ref[h] = w.astype(bf16)
        u_ref[h] = u.astype(bf16)
        step = -dot(w, k, TN)
        add = dot(u, k, TN)
        groups, rows_each = send_ref.shape[1], send_ref.shape[2] - HEAD_DIM
        for g in range(groups):
            send_ref[h, g, 0:HEAD_DIM, :] = step.astype(bf16)
            send_ref[h, g, HEAD_DIM:, :] = add[g * rows_each : (g + 1) * rows_each].astype(bf16)


def chain_kernel(blocks, recv_ref, out_ref):
    state = jnp.zeros(out_ref.shape[1:], f32)
    for d in range(blocks):
        high, low = split(state)
        out_ref[d] = high
        if d < blocks - 1:
            step = recv_ref[d, 0:HEAD_DIM, :]
            add = recv_ref[d, HEAD_DIM:, :].astype(f32)
            state = state + add + (dot(high, step) + dot(low, step))


def back_chain_kernel(blocks, recv_ref, add_ref, out_ref):
    state = jnp.zeros(out_ref.shape[1:], f32)
    for d in range(blocks - 1, -1, -1):
        high, low = split(state)
        out_ref[d] = high
        if d > 0:
            step = recv_ref[d, 0:HEAD_DIM, :]
            add = add_ref[d].astype(f32)
            state = state + add + (dot(high, step, NT) + dot(low, step, NT))


def mixer_kernel(
    heads, state_ref, q_ref, w_ref, u_ref, score_ref, gain_ref, mask_ref, out_ref, x_ref, mix_ref
):
    a, b = slice(0, HALF), slice(HALF, 2 * HALF)
    mask = mask_ref[0]
    for h in range(heads):
        lanes = slice(h * HEAD_DIM, (h + 1) * HEAD_DIM)
        state = state_ref[h]
        x = u_ref[h].astype(f32) - dot(w_ref[h], state, NT)
        x_ref[h] = x.astype(bf16)
        base = dot(q_ref[h], state, NT)
        top = dot(score_ref[h, 0], x[a])
        bottom = dot(score_ref[h, 1], x[a]) + dot(score_ref[h, 2], x[b])
        mixer = base + jnp.concatenate([top, bottom], axis=0)
        mix_ref[h] = mixer
        inv = lax.rsqrt(jnp.mean(mixer * mixer, axis=1, keepdims=True) + EPS)
        out_ref[0, :, lanes] = (mixer * inv * gain_ref[...] * mask).astype(bf16)


def head_back_kernel(
    heads, grad_ref, mix_ref, gain_ref, mask_ref, q_ref, w_ref, score_ref,
    send_ref, dmix_ref, dx_ref, dgain_ref,
):
    a, b = slice(0, HALF), slice(HALF, 2 * HALF)
    mask = mask_ref[0]
    gain = gain_ref[...]
    for h in range(heads):
        lanes = slice(h * HEAD_DIM, (h + 1) * HEAD_DIM)
        grad = grad_ref[0, :, lanes].astype(f32) * mask
        mixer = mix_ref[h]
        inv = lax.rsqrt(jnp.mean(mixer * mixer, axis=1, keepdims=True) + EPS)
        scaled = mixer * inv
        dgain_ref[h] = jnp.sum(grad * scaled, axis=0, keepdims=True)
        inner = jnp.mean(gain * grad * scaled, axis=1, keepdims=True)
        dmix = inv * (gain * grad - scaled * inner)
        dmix_ref[h] = dmix.astype(bf16)
        top = dot(score_ref[h, 0], dmix[a], TN) + dot(score_ref[h, 1], dmix[b], TN)
        bottom = dot(score_ref[h, 2], dmix[b], TN)
        dx = jnp.concatenate([top, bottom], axis=0)
        dx_ref[h] = dx
        send_ref[h] = (dot(dmix, q_ref[h], TN) - dot(dx, w_ref[h], TN)).astype(bf16)


def span_back_kernel(
    heads, proj_ref, halo_ref, conv_ref, strength_ref, state_ref, dstate_ref,
    x_ref, dmix_ref, dx_ref, gram_ref, inv_ref,
    dproj_ref, tail_ref, ahead_ref, dlogit_ref, dconv_ref, rows, grads,
):
    lower, lower_diag = masks()
    a, b = slice(0, HALF), slice(HALF, 2 * HALF)
    length = proj_ref.shape[2]
    lane = lax.broadcasted_iota(jnp.int32, strength_ref.shape[1:], 1)
    dlogit = jnp.zeros(strength_ref.shape[1:], f32)
    for h in range(heads):
        lanes = slice(h * HEAD_DIM, (h + 1) * HEAD_DIM)
        mixed, sig, active = [], [], []
        for j in range(3):
            mixed.append(conv_rows(j, proj_ref, halo_ref, conv_ref, rows.at[h * 3 + j], lanes))
            sig.append(sigmoid(mixed[j]))
            active.append(mixed[j] * sig[j])
        q_inv = lax.rsqrt(jnp.sum(active[0] * active[0], axis=1, keepdims=True) + EPS)
        k_inv = lax.rsqrt(jnp.sum(active[1] * active[1], axis=1, keepdims=True) + EPS)
        q, k, v = active[0] * q_inv, active[1] * k_inv, active[2]
        kb = k.astype(bf16)
        beta = column_of(strength_ref[0], h)
        state, dstate = state_ref[h], dstate_ref[h]
        x, dmix = x_ref[h], dmix_ref[h]
        gaa, gba, gbb = gram_ref[h, 0], gram_ref[h, 1], gram_ref[h, 2]
        dx = dx_ref[h] + dot(kb, dstate, NT)
        y_b = dot(inv_ref[h, 1], dx[b], TN)
        y_a = dot(inv_ref[h, 0], dx[a] - dot(gba, beta[b] * y_b, TN), TN)
        y = jnp.concatenate([y_a, y_b], axis=0)
        inner = jnp.concatenate([dot(gaa, x[a]), dot(gba, x[a]) + dot(gbb, x[b])], axis=0)
        residual = v - dot(kb, state, NT) - inner
        dbeta = jnp.sum(y * residual, axis=1, keepdims=True)
        dlogit = jnp.where(lane == h, dbeta * beta * (1.0 - beta), dlogit)
        dv = beta * y
        dgram = -dot(dv, x, NT)
        dscore = dot(dmix, x, NT)
        dg_aa = jnp.where(lower, dgram[a, a], 0.0).astype(bf16)
        dg_bb = jnp.where(lower, dgram[b, b], 0.0).astype(bf16)
        dg_ba = dgram[b, a].astype(bf16)
        ds_aa = jnp.where(lower_diag, dscore[a, a], 0.0).astype(bf16)
        ds_bb = jnp.where(lower_diag, dscore[b, b], 0.0).astype(bf16)
        ds_ba = dscore[b, a].astype(bf16)
        qb = q.astype(bf16)
        dq = dot(dmix, state) + jnp.concatenate(
            [dot(ds_aa, kb[a]), dot(ds_ba, kb[a]) + dot(ds_bb, kb[b])], axis=0
        )
        dk = dot(x, dstate) - dot(dv, state)
        dk_a = (
            dot(ds_aa, qb[a], TN) + dot(ds_ba, qb[b], TN)
            + dot(dg_aa, kb[a]) + dot(dg_aa, kb[a], TN) + dot(dg_ba, kb[b], TN)
        )
        dk_b = (
            dot(ds_bb, qb[b], TN) + dot(dg_ba, kb[a])
            + dot(dg_bb, kb[b]) + dot(dg_bb, kb[b], TN)
        )
        dk = dk + jnp.concatenate([dk_a, dk_b], axis=0)
        dact = [
            (dq - q * jnp.sum(q * dq, axis=1, keepdims=True)) * q_inv,
            (dk - k * jnp.sum(k * dk, axis=1, keepdims=True)) * k_inv,
            dv,
        ]
        for j in range(3):
            dmixed = dact[j] * sig[j] * (1.0 + mixed[j] * (1.0 - sig[j]))
            own = rows.at[h * 3 + j]
            pad = grads.at[h * 3 + j]
            pad[0:HALO, :] = jnp.zeros((HALO, HEAD_DIM), f32)
            pad[HALO : HALO + length, :] = dmixed
            pad[HALO + length :, :] = jnp.zeros((HALO, HEAD_DIM), f32)
            whole = None
            for i in range(CONV):
                start = HALO - (CONV - 1) + i
                dconv_ref[j, 0, i : i + 1, lanes] = jnp.sum(
                    dmixed * own[start : start + length, :], axis=0, keepdims=True
                )
                shift = CONV - 1 - i
                term = conv_ref[j, i : i + 1, lanes] * pad[shift : shift + HALO + length, :]
                whole = term if whole is None else whole + term
            ahead_ref[j, 0, :, lanes] = whole[0:HALO].astype(bf16)
            dproj_ref[j, 0, :, lanes] = whole[HALO:].astype(bf16)
            tail_ref[j, 0, :, lanes] = whole[length:]
    dlogit_ref[0] = dlogit


def kernel_params():
    return pltpu.CompilerParams(vmem_limit_bytes=48 * 1024 * 1024)


def spec(block, index):
    return pl.BlockSpec(block, index)


def mixer_calls(seqs, length, heads):
    chains = seqs * heads
    width = heads * HEAD_DIM
    at = {
        "proj": spec((3, 1, length, width), lambda s: (0, s, 0, 0)),
        "halo": spec((3, 1, HALO, width), lambda s: (0, s, 0, 0)),
        "conv": spec((3, CONV, width), lambda s: (0, 0, 0)),
        "strength": spec((1, length, heads), lambda s: (s, 0, 0)),
        "tokens": spec((heads, length, HEAD_DIM), lambda s: (s, 0, 0)),
        "state": spec((heads, HEAD_DIM, HEAD_DIM), lambda s: (s, 0, 0)),
        "three": spec((heads, 3, HALF, HALF), lambda s: (s, 0, 0, 0)),
        "two": spec((heads, 2, HALF, HALF), lambda s: (s, 0, 0, 0)),
        "rows": spec((1, length, width), lambda s: (s, 0, 0)),
        "mask": spec((1, length, 1), lambda s: (s, 0, 0)),
        "gain": spec((1, HEAD_DIM), lambda s: (0, 0)),
    }
    shape = {
        "tokens": lambda kind: jax.ShapeDtypeStruct((chains, length, HEAD_DIM), kind),
        "three": jax.ShapeDtypeStruct((chains, 3, HALF, HALF), bf16),
        "two": jax.ShapeDtypeStruct((chains, 2, HALF, HALF), bf16),
    }
    return at, shape


def from_behind(value, axis, steps):
    count = lax.axis_size(axis)
    initial, last = (max(0, -steps), min(count, count - steps))
    return lax.ppermute(value, axis, [(source, source + steps) for source in range(initial, last)])


def exchange(blocks, axis):
    return lax.all_to_all(blocks, axis, 0, 0)


def gather_columns(own):
    count = lax.axis_size("head")
    parts = exchange(jnp.broadcast_to(own[None], (count,) + own.shape), "head")
    return jnp.moveaxis(parts, 0, 2).reshape(own.shape[:2] + (count * own.shape[2],))


def scatter_sum(partial_rows):
    count = lax.axis_size("head")
    seqs, length, columns = partial_rows.shape
    parts = jnp.moveaxis(partial_rows.reshape(seqs, length, count, columns // count), 2, 0)
    return jnp.sum(exchange(parts, "head").astype(f32), axis=0)


def row_scale(rows):
    return lax.rsqrt(jnp.mean(rows * rows, axis=-1, keepdims=True) + EPS)


def shards(
    tokens,
    lengths,
    norm_gain,
    query_key_value_weight,
    strength_projection,
    conv_weight,
    head_gain,
    output_projection,
    mlp_gain,
    gate_up_weight,
    down_projection,
    out_grad,
):
    seqs, length, width = tokens.shape
    model = norm_gain.shape[0]
    heads = width // HEAD_DIM
    chains = seqs * heads
    blocks = lax.axis_size("seq")
    groups = blocks // chains
    cols = HEAD_DIM // groups
    hidden = down_projection.shape[0]
    col_start = lax.axis_index("head") * width
    positions = lax.axis_index("seq") * length + jnp.arange(length, dtype=jnp.int32)
    mask = (positions[None, :] < lengths[:, None]).astype(f32)[:, :, None]
    at, shape = mixer_calls(seqs, length, heads)
    gain_row = head_gain[None, :]

    full = gather_columns(tokens)
    grad_rows = lax.all_gather(out_grad, "head", axis=2, tiled=True)
    full32 = full.astype(f32)
    in_scale = row_scale(full32)
    normed_in = (full32 * in_scale * norm_gain).astype(bf16)
    projected = jnp.einsum(
        "pit,ftw->fpiw", normed_in, query_key_value_weight, preferred_element_type=f32
    ).astype(bf16)
    logits = jnp.einsum(
        "qbx,xg->qbg", normed_in, strength_projection, preferred_element_type=f32
    )
    strength = jax.nn.sigmoid(logits) * mask
    halo = from_behind(projected[:, :, length - HALO :, :], "seq", 1)

    send, q, k, v, w, u, gram, score, inv = pl.pallas_call(
        partial(span_kernel, heads),
        grid=(seqs,),
        in_specs=[at["proj"], at["halo"], at["conv"], at["strength"]],
        out_specs=[
            spec((heads, groups, HEAD_DIM + cols, HEAD_DIM), lambda s: (s, 0, 0, 0)),
            at["tokens"], at["tokens"], at["tokens"], at["tokens"], at["tokens"],
            at["three"], at["three"], at["two"],
        ],
        out_shape=[
            jax.ShapeDtypeStruct((chains, groups, HEAD_DIM + cols, HEAD_DIM), bf16),
            *[shape["tokens"](bf16)] * 5,
            shape["three"], shape["three"], shape["two"],
        ],
        scratch_shapes=[pltpu.VMEM((heads * 3, HALO + length, HEAD_DIM), f32)],
        compiler_params=kernel_params(),
    )(projected, halo, conv_weight, strength)

    received = exchange(send.reshape(blocks, HEAD_DIM + cols, HEAD_DIM), "seq")
    entering = pl.pallas_call(
        partial(chain_kernel, blocks),
        out_shape=jax.ShapeDtypeStruct((blocks, cols, HEAD_DIM), bf16),
        compiler_params=kernel_params(),
    )(received)
    state = exchange(entering, "seq").reshape(chains, HEAD_DIM, HEAD_DIM)

    head_out, x, mixer = pl.pallas_call(
        partial(mixer_kernel, heads),
        grid=(seqs,),
        in_specs=[
            at["state"], at["tokens"], at["tokens"], at["tokens"], at["three"], at["gain"],
            at["mask"],
        ],
        out_specs=[at["rows"], at["tokens"], at["tokens"]],
        out_shape=[
            jax.ShapeDtypeStruct((seqs, length, width), bf16),
            shape["tokens"](bf16),
            shape["tokens"](f32),
        ],
        compiler_params=kernel_params(),
    )(state, q, w, u, score, gain_row, mask)

    branch = jnp.einsum("rpj,jk->rpk", head_out, output_projection, preferred_element_type=f32)
    middle_own = tokens.astype(f32) + scatter_sum(branch.astype(bf16))
    middle = gather_columns(middle_own.astype(bf16)).astype(f32)
    mid_scale = row_scale(middle)
    normed_mid = (middle * mid_scale * mlp_gain).astype(bf16)

    gated = jnp.einsum("rux,gxt->grut", normed_mid, gate_up_weight, preferred_element_type=f32)
    gate_sig = jax.nn.sigmoid(gated[0])
    gate_act = gated[0] * gate_sig
    features = (gate_act * gated[1]).astype(bf16)
    feed = jnp.einsum("yqj,jo->yqo", features, down_projection, preferred_element_type=f32)
    feed_own = lax.psum_scatter(
        feed.astype(bf16), "head", scatter_dimension=2, tiled=True
    ).astype(f32)
    output = (middle_own + feed_own).astype(bf16)
    hidden_grad = jnp.einsum("zxp,hp->zxh", grad_rows, down_projection, preferred_element_type=f32)
    gate_grad = hidden_grad * gated[1] * gate_sig * (1.0 + gated[0] * (1.0 - gate_sig))
    up_grad = hidden_grad * gate_act
    gated_grad = jnp.stack([gate_grad, up_grad]).astype(bf16)
    mid_part = jnp.einsum("nyqp,ngp->yqg", gated_grad, gate_up_weight, preferred_element_type=f32)
    mid_grad_own = scatter_sum(mid_part.astype(bf16))
    mid_grad = gather_columns(mid_grad_own.astype(bf16)).astype(f32)

    gate_up_part = jnp.einsum("qig,kqiv->gkv", normed_mid, gated_grad, preferred_element_type=f32)
    down_part = jnp.einsum("rtx,rtq->xq", grad_rows, features, preferred_element_type=f32)
    feed_part = jnp.concatenate(
        [gate_up_part.reshape(model, 2 * hidden).astype(bf16), down_part.astype(bf16)], axis=1
    )
    feed_sum = lax.psum_scatter(feed_part, "seq", scatter_dimension=0, tiled=True).astype(f32)

    mid_dot = jnp.mean(mlp_gain * mid_grad * middle, axis=-1, keepdims=True)
    middle_grad = grad_rows.astype(f32) + (
        mid_scale * mlp_gain * mid_grad - mid_scale * mid_scale * mid_scale * middle * mid_dot
    )
    branch_grad = middle_grad.astype(bf16)
    own_gain = lax.dynamic_slice_in_dim(mlp_gain, col_start, width, 0)
    middle_grad_own = out_grad.astype(f32) + (
        mid_scale * own_gain * mid_grad_own
        - mid_scale * mid_scale * mid_scale * middle_own * mid_dot
    )
    mlp_gain_part = jnp.sum(mid_grad_own * middle_own * mid_scale, axis=(0, 1))
    head_grad = jnp.einsum(
        "hpj,wj->hpw", branch_grad, output_projection, preferred_element_type=f32
    ).astype(bf16)

    send_back, dmix, dx, dgain = pl.pallas_call(
        partial(head_back_kernel, heads),
        grid=(seqs,),
        in_specs=[
            at["rows"], at["tokens"], at["gain"], at["mask"], at["tokens"], at["tokens"],
            at["three"],
        ],
        out_specs=[
            at["state"], at["tokens"], at["tokens"],
            spec((heads, 1, HEAD_DIM), lambda s: (s, 0, 0)),
        ],
        out_shape=[
            jax.ShapeDtypeStruct((chains, HEAD_DIM, HEAD_DIM), bf16),
            shape["tokens"](bf16),
            shape["tokens"](f32),
            jax.ShapeDtypeStruct((chains, 1, HEAD_DIM), f32),
        ],
        compiler_params=kernel_params(),
    )(head_grad, mixer, gain_row, mask, q, w, score)

    added = exchange(send_back.reshape(blocks, cols, HEAD_DIM), "seq")
    leaving = pl.pallas_call(
        partial(back_chain_kernel, blocks),
        out_shape=jax.ShapeDtypeStruct((blocks, cols, HEAD_DIM), bf16),
        compiler_params=kernel_params(),
    )(received, added)
    dstate = exchange(leaving, "seq").reshape(chains, HEAD_DIM, HEAD_DIM)

    dproj, tail, ahead, dlogit, dconv = pl.pallas_call(
        partial(span_back_kernel, heads),
        grid=(seqs,),
        in_specs=[
            at["proj"], at["halo"], at["conv"], at["strength"], at["state"], at["state"],
            at["tokens"], at["tokens"], at["tokens"], at["three"], at["two"],
        ],
        out_specs=[
            at["proj"], at["halo"], at["halo"], at["strength"],
            spec((3, 1, CONV, width), lambda s: (0, s, 0, 0)),
        ],
        out_shape=[
            jax.ShapeDtypeStruct((3, seqs, length, width), bf16),
            jax.ShapeDtypeStruct((3, seqs, HALO, width), f32),
            jax.ShapeDtypeStruct((3, seqs, HALO, width), bf16),
            jax.ShapeDtypeStruct((seqs, length, heads), f32),
            jax.ShapeDtypeStruct((3, seqs, CONV, width), f32),
        ],
        scratch_shapes=[
            pltpu.VMEM((heads * 3, HALO + length, HEAD_DIM), f32),
            pltpu.VMEM((heads * 3, 2 * HALO + length, HEAD_DIM), f32),
        ],
        compiler_params=kernel_params(),
    )(projected, halo, conv_weight, strength, state, dstate, x, dmix, dx, gram, inv)

    sent_back = from_behind(ahead, "seq", -1).astype(f32)
    proj_grad = lax.dynamic_update_slice_in_dim(
        dproj, (tail + sent_back).astype(bf16), length - HALO, 2
    )
    logit_grad = dlogit.astype(bf16)

    in_part = jnp.einsum(
        "qxtm,qbm->xtb", proj_grad, query_key_value_weight, preferred_element_type=f32
    ) + jnp.einsum("xzi,pi->xzp", logit_grad, strength_projection, preferred_element_type=f32)
    in_dot_part = jnp.mean(norm_gain * in_part * full32, axis=-1, keepdims=True)
    in_dot, head_gain_part = lax.psum((in_dot_part, jnp.sum(dgain, axis=(0, 1))), "head")
    in_grad = scatter_sum(in_part.astype(bf16))
    own = tokens.astype(f32)
    in_gain = lax.dynamic_slice_in_dim(norm_gain, col_start, width, 0)
    tokens_grad = (
        in_scale * in_gain * in_grad - in_scale * in_scale * in_scale * own * in_dot
        + middle_grad_own
    ).astype(bf16)
    norm_gain_part = jnp.sum(in_grad * own * in_scale, axis=(0, 1))

    qkv_part = jnp.einsum("kub,hkuy->bhy", normed_in, proj_grad, preferred_element_type=f32)
    out_part = jnp.einsum("gmv,gmx->vx", branch_grad, head_out, preferred_element_type=f32)
    strength_part = jnp.einsum("qrg,qre->ge", normed_in, logit_grad, preferred_element_type=f32)
    mix_part = jnp.concatenate(
        [
            qkv_part.reshape(model, 3 * width).astype(bf16),
            out_part.astype(bf16),
            jnp.pad(strength_part.astype(bf16), ((0, 0), (0, HEAD_DIM - heads))),
        ],
        axis=1,
    )
    mix_sum = lax.psum_scatter(mix_part, "seq", scatter_dimension=0, tiled=True).astype(f32)
    small = jnp.concatenate(
        [
            jnp.sum(dconv, axis=1).reshape(3 * CONV, width),
            norm_gain_part[None],
            mlp_gain_part[None],
            jnp.pad(head_gain_part[None], ((0, 0), (0, width - HEAD_DIM))),
        ]
    ).astype(bf16)
    small_sum = lax.psum(small, "seq").astype(f32)
    mine = lax.axis_index("seq")
    each = width // blocks
    own_small = lax.dynamic_slice_in_dim(small_sum[: 3 * CONV + 2], mine * each, each, 1)
    gain_each = HEAD_DIM // blocks
    head_gain_own = lax.dynamic_slice_in_dim(
        small_sum[3 * CONV + 2], mine * gain_each, gain_each, 0
    )
    rows_own = model // blocks
    qkv_grad = jnp.moveaxis(mix_sum[:, : 3 * width].reshape(rows_own, 3, width), 1, 0)
    return (
        output,
        tokens_grad,
        own_small[3 * CONV],
        qkv_grad,
        mix_sum[:, 4 * width : 4 * width + heads],
        own_small[: 3 * CONV].reshape(3, CONV, each),
        head_gain_own,
        mix_sum[:, 3 * width : 4 * width].T,
        own_small[3 * CONV + 1],
        jnp.moveaxis(feed_sum[:, : 2 * hidden].reshape(rows_own, 2, hidden), 1, 0),
        feed_sum[:, 2 * hidden :].T,
    )


def solution(mesh):
    return jax.shard_map(
        shards,
        mesh=mesh,
        in_specs=(
            P(None, "seq", "head"),
            P(),
            P(),
            P(None, None, "head"),
            P(None, "head"),
            P(None, None, "head"),
            P(),
            P("head", None),
            P(),
            P(None, None, "head"),
            P("head", None),
            P(None, "seq", "head"),
        ),
        out_specs=(
            P(None, "seq", "head"),
            P(None, "seq", "head"),
            P(("head", "seq")),
            P(None, "seq", "head"),
            P("seq", "head"),
            P(None, None, ("head", "seq")),
            P("seq"),
            P("head", "seq"),
            P(("head", "seq")),
            P(None, "seq", "head"),
            P("head", "seq"),
        ),
        check_vma=False,
    )
```

time: 1930 us -> 664 us (0.34)
  waiting for transfers between devices: 685 us -> 98.2 us
  other arithmetic: 559 us -> 48.4 us
  matrix products: 428 us -> 83.5 us
  blocking collectives: 78 us -> 238 us
  local copies, waits for them, and re-layouts: 144 us -> 65.9 us
  Pallas kernels: 0 us -> 64.9 us
  starting transfers between devices: 4.5 us -> 42.4 us
    another operation x45 -> x1, other arithmetic: 488 us -> 3.44 us  [the longest x32 488 us: one_block(): lax.linalg.triangular_solve(system, right_side, left_side=True, lower=True)]
    dot_general x216 -> x15, matrix products: 398 us -> 83.5 us  [the longest x1 11.3 us: shards(): jnp.einsum('rux,gxt->grut', normed_mid, gate_up_weight, preferred_element...]
    psum x3 -> x0, waiting for transfers between devices: 266 us -> none  [the longest x1 149 us: shards(): middle_rows = full_rows + lax.psum(attention_portion, 'head')]
    all_gather x7 -> x1, waiting for transfers between devices: 225 us -> 0.01 us  [shards(): grad_rows = lax.all_gather(out_grad, 'head', axis=2, tiled=True)]
    unnamed x19 -> x5, waiting for transfers between devices: 167 us -> 0.76 us
    psum x1 -> x2, blocking collectives: 9.58 us -> 152 us  [the longest x1 126 us: shards(): small_sum = lax.psum(small, 'seq').astype(f32)]
    all_to_all x0 -> x7, waiting for transfers between devices: none -> 95.6 us  [exchange(): return lax.all_to_all(blocks, axis, 0, 0)]
    all_to_all x0 -> x3, blocking collectives: none -> 86.3 us  [exchange(): return lax.all_to_all(blocks, axis, 0, 0)]
  transfers between devices with their start and end apart: 18 -> 13, of which waited for: 11 -> 8; matrix products, arithmetic and copies ran while one was open for 43% -> 18% of each run, Pallas kernels for 0% -> 3%
where the time goes in v1:
time: 664 us; the launch traced here: 657 us
  blocking collectives  238 us (36%)
  waiting for transfers between devices  98.2 us (15%)
  matrix products  83.5 us (13%)
  local copies, waits for them, and re-layouts  65.9 us (10%)
  Pallas kernels  64.9 us (10%)
  other arithmetic  48.4 us (7%)
  starting transfers between devices  42.4 us (6%)
  between operations  14.8 us (2%)
    psum x1, blocking collectives, shards(): small_sum = lax.psum(small, 'seq').astype(f32)  126 us
    all_to_all x7, waiting for transfers between devices, exchange(): return lax.all_to_all(blocks, axis, 0, 0)  95.6 us
    all_to_all x3, blocking collectives, exchange(): return lax.all_to_all(blocks, axis, 0, 0)  86.3 us
    all_to_all x7, starting transfers between devices, exchange(): return lax.all_to_all(blocks, axis, 0, 0)  38.7 us
    pallas_call x1, Pallas kernels, shards(): pl.pallas_call(partial(span_kernel, heads), grid=(seqs,), in_specs=[at['p...  36.8 us
    unnamed x141, local copies, waits for them, and re-layouts  34.7 us
    psum x1, blocking collectives, shards(): lax.psum((in_dot_part, jnp.sum(dgain, axis=(0, 1))), 'head')  26.2 us
  transfers between devices with their start and end apart: 13, of which 8 were waited for; matrix products, arithmetic and copies ran while one was open for 18% of the time, Pallas kernels for 3%

profile of v1, /device:TPU:2, one launch (start us, length us, event | category | flops | bytes accessed | tf_op | source)
XLA Modules:
  0.0 656.6 jit_solution(1747671811129242899)
XLA Ops:
  7.2 2.7 broadcast_in_dim.17
  10.0 4.9 all-to-all-start
  14.9 25.1 %all-to-all-done = bf16[4,2,256,512]{3,2,1,0:T(8,128)(2,1)} async-done(((bf16[4,2,256,512]{3,2,1,0:T(8,128)(2,1)}), bf16[4,2,256,512]{3,2,1,0:T(8,128)(2,1)}, u32[]{:S(2)}, u32[]{:S(2)}) %all-to-all-start) | async-done | bytes 2097184 | tf_op jit(solution)/shard_map/all_to_all | solution.py:321
  40.0 4.1 copy.95
  44.1 2.2 multiply_reduce_fusion.1
  46.3 2.4 convert_element_type.221
  49.3 5.4 copy.131
  54.7 2.6 multiply_convert_fusion.2
  57.4 7.0 %fusion.39.proj_ref = bf16[3,2,256,512]{3,2,1,0:T(8,128)(2,1)S(1)} fusion(bf16[3,2048,512]{2,1,0:T(8,128)(2,1)} %param.15, bf16[2,256,2048]{2,1,0:T(8,128)(2,1)S(1)} %multiply_convert_fusion.2), kind=kOutput, calls=%fused_computation.66 | convolution fusion | flops 3222011904 | bytes 9961472 | tf_op jit(solution)/shard_map/pit,ftw->fpiw/dot_general | solution.py:374
  64.4 1.6 collective-permute-start
  66.7 36.8 %shard_map.203 = (bf16[8,4,160,128]{3,2,1,0:T(8,128)(2,1)}, bf16[8,256,128]{2,1,0:T(8,128)(2,1)S(1)}, bf16[8,256,128]{2,1,0:T(8,128)(2,1)}, bf16[8,256,128]{2,1,...) custom-call(bf16[3,2,256,512]{3,2,1,0:T(8,128)(2,1)} %copy-done.42, ...), custom_call_target="tpu_custom_call" | custom-call | tf_op jit(solution)/shard_map/pallas_call | solution.py:383
  107.0 31.8 %all_to_all.50.recv_ref = bf16[32,160,128]{2,1,0:T(8,128)(2,1)S(1)} all-to-all(bf16[32,160,128]{2,1,0:T(8,128)(2,1)} %bitcast.213), channel_id=1, replica_groups=mesh['seq'=32,'head'=4] {'seq'}, dimensions={0} | all-to-all | bytes 2621440 | tf_op jit(solution)/shard_map/all_to_all | solution.py:321
  138.8 4.2 shard_map.204
  143.7 4.6 all-to-all-start.2
  149.2 8.0 %all-to-all-done.2 = bf16[32,32,128]{2,1,0:T(8,128)(2,1)} async-done(((bf16[32,32,128]{2,1,0:T(8,128)(2,1)}), bf16[32,32,128]{2,1,0:T(8,128)(2,1)}, u32[]{:S(2)}, u32[]{:S(2)}) %all-to-all-start.2) | async-done | bytes 262176 | tf_op jit(solution)/shard_map/all_to_all | solution.py:321
  162.4 2.5 shard_map.205
  165.0 1.3 convolution_convert_fusion
  166.5 29.9 %all_to_all.51 = bf16[4,2,256,512]{3,2,1,0:T(8,128)(2,1)S(1)} all-to-all(bf16[4,2,256,512]{3,2,1,0:T(8,128)(2,1)S(1)} %bitcast.203), channel_id=1, replica_groups=mesh['seq'=32,'head'=4] {'head'}, dimensions={0} | all-to-all | bytes 4194304 | tf_op jit(solution)/shard_map/all_to_all | solution.py:321
  197.9 1.5 broadcast_in_dim.19
  199.4 5.9 all-to-all-start.4
  206.0 36.9 %all-to-all-done.4 = bf16[4,2,256,512]{3,2,1,0:T(8,128)(2,1)} async-done(((bf16[4,2,256,512]{3,2,1,0:T(8,128)(2,1)}), bf16[4,2,256,512]{3,2,1,0:T(8,128)(2,1)}, u32[]{:S(2)}, u32[]{:S(2)}) %all-to-all-start.4) | async-done | bytes 2097184 | tf_op jit(solution)/shard_map/all_to_all | solution.py:321
  242.8 2.2 convert_bitcast_fusion
  245.5 3.6 fusion.18
  249.2 11.3 %fusion.15 = f32[2,2,256,1408]{3,2,0,1:T(8,128)} fusion(bf16[2,2048,1408]{2,1,0:T(8,128)(2,1)} %param.21, f32[2,256,2048]{2,1,0:T(8,128)S(1)} %bitcast.196, f32[2048]{0:T(1024)S(1)} %copy-done.55, f32[2,256]{1,0:T(2,128)S(1)} %get-tuple-element.120), kind=kOutput, calls=%fused_computation.25 | convolution fusion | flops 5908725760 | bytes 21506048 | tf_op jit(solution)/shard_map/rux,gxt->grut/dot_general | solution.py:431
  260.5 10.3 %fusion.45 = (bf16[1,2,256,1408]{3,2,1,0:T(8,128)(2,1)S(1)}, bf16[1,2,256,1408]{3,2,1,0:T(8,128)(2,1)S(1)}, bf16[2,256,1408]{2,1,0:T(8,128)(2,1)}) fusion(f32[2,2,256,1408]{3,2,0,1:T(8,128)} %fusion.15, bf16[2,256,2048]{2,1,0:T(8,128)(2,1)} %all-gather.2.cloned.1.call-done, bf16[1408,2048]{1,0:T(8,128)(2,1)} %param.22), kind=kOutput, calls=%fused_computation.68 | convolution fusion | flops 2963603456 | bytes 17956864 | tf_op jit(solution)/shard_map/zxp,hp->zxh/dot_general | solution.py:440
  270.8 10.1 %bitcast_convert_fusion.4 = bf16[2,256,2048]{2,1,0:T(8,128)(2,1)S(1)} fusion(bf16[2,2048,1408]{2,1,0:T(8,128)(2,1)} %param.21, bf16[1,2,256,1408]{3,2,1,0:T(8,128)(2,1)S(1)} %get-tuple-element.109, bf16[1,2,256,1408]{3,2,1,0:T(8,128)(2,1)S(1)} %get-tuple-element.108), kind=kOutput, calls=%fused_computation.30 | convolution fusion | flops 5908070400 | bytes 16515072 | tf_op jit(solution)/shard_map/nyqp,ngp->yqg/dot_general | solution.py:444
  281.1 24.7 %all_to_all.52 = bf16[4,2,256,512]{3,2,1,0:T(8,128)(2,1)S(1)} all-to-all(bf16[4,2,256,512]{3,2,1,0:T(8,128)(2,1)S(1)} %bitcast.204), channel_id=1, replica_groups=mesh['seq'=32,'head'=4] {'head'}, dimensions={0} | all-to-all | bytes 4194304 | tf_op jit(solution)/shard_map/all_to_all | solution.py:321
  307.1 1.6 broadcast_in_dim.20
  308.7 5.9 all-to-all-start.6
  315.0 7.8 %fusion.22 = bf16[2,256,2048]{2,1,0:T(8,128)(2,1)} fusion(bf16[2,256,1408]{2,1,0:T(8,128)(2,1)} %get-tuple-element.112, bf16[1408,2048]{1,0:T(8,128)(2,1)} %param.22), kind=kOutput, calls=%fused_computation.41 | convolution fusion | flops 2953838592 | bytes 9306112 | tf_op jit(solution)/shard_map/yqj,jo->yqo/dot_general | solution.py:435
  322.8 15.9 %all-to-all-done.6 = bf16[4,2,256,512]{3,2,1,0:T(8,128)(2,1)} async-done(((bf16[4,2,256,512]{3,2,1,0:T(8,128)(2,1)}), bf16[4,2,256,512]{3,2,1,0:T(8,128)(2,1)}, u32[]{:S(2)}, u32[]{:S(2)}) %all-to-all-start.6) | async-done | bytes 2097184 | tf_op jit(solution)/shard_map/all_to_all | solution.py:321
  338.7 3.0 fusion.19
  341.8 2.2 convert_bitcast_fusion.1
  344.7 1.6 copy-done.34
  348.1 1.3 fusion.46.grad_ref
  350.7 4.0 shard_map.206
  355.5 7.4 %all-to-all-start.7 = ((bf16[32,32,128]{2,1,0:T(8,128)(2,1)}), bf16[32,32,128]{2,1,0:T(8,128)(2,1)S(1)}, u32[]{:S(2)}, u32[]{:S(2)}) async-start(bf16[32,32,128]{2,1,0:T(8,128)(2,1)} %bitcast.26), calls=%async_computation.8 | async-start | bytes 524288 | tf_op jit(solution)/shard_map/all_to_all | solution.py:321
  362.9 3.4 multiply_convert_fusion
  366.3 5.5 all-to-all-done.7.add_ref
  371.8 5.5 shard_map.207
  377.2 3.9 all-to-all-start.8
  381.4 4.4 bitcast_convert_fusion.3
  385.8 4.2 all-to-all-done.8
  392.1 11.9 %shard_map.208 = (bf16[3,2,256,512]{3,2,1,0:T(8,128)(2,1)}, f32[3,2,8,512]{3,2,1,0:T(8,128)S(1)}, bf16[3,2,8,512]{3,2,1,0:T(8,128)(2,1)S(1)}, f32[2,256,4]{2,1,0:T(8,128)S(1)}, f32[3,2,4,512]{3,2,1,0:T(4,128)S(1)}) custom-call(bf16[3,2,256,512]{3,2,1,0:T(8,128)(2,1)} %copy-done.42, bf16[3,2,8,512]{3,2,1,0:T(8,128)(2,1)S(1)} %collective-permute-done.halo_ref, ...), custom_call_target="tpu_custom_call" | custom-call | tf_op jit(solution)/shard_map/pallas_call | solution.py:498
  404.0 1.3 collective-permute-start.1
  405.7 1.4 collective-permute-done.1
  407.8 1.7 copy.108
  409.5 5.4 bitcast_convert_fusion.1
  415.0 4.3 fusion.5
  419.3 11.7 %copy.133 = bf16[2048,2176]{1,0:T(8,128)(2,1)} copy(bf16[2048,2176]{0,1:T(8,128)(2,1)} %fusion.5) | data formatting | bytes 17825792
  432.8 1.9 fusion.32
  434.7 4.7 copy.113
  439.4 7.7 %fusion.6 = bf16[2048,1408]{1,0:T(8,128)(2,1)} fusion(bf16[2,256,1408]{2,1,0:T(8,128)(2,1)S(1)} %copy-done.68, bf16[2,256,2048]{2,1,0:T(8,128)(2,1)} %all-gather.2.cloned.1.call-done), kind=kOutput, calls=%fused_computation.11 | convolution fusion | flops 2955673600 | bytes 9306112 | tf_op jit(solution)/shard_map/rtx,rtq->xq/dot_general | solution.py:449
  447.2 8.8 %bitcast_convert_fusion = bf16[2048,2816]{1,0:T(8,128)(2,1)S(1)} fusion(bf16[2816,256,2]{1,0,2:T(8,128)(2,1)} %bitcast.206, f32[2,256,2048]{2,1,0:T(8,128)S(1)} %bitcast.198, f32[2048]{0:T(1024)S(1)} %copy-done.55, f32[2,256]{1,0:T(2,128)S(1)} %copy-done.61), kind=kOutput, calls=%fused_computation | convolution fusion | flops 5914492928 | bytes 18622464 | tf_op jit(solution)/shard_map/qig,kqiv->gkv/dot_general | solution.py:448
  456.0 10.0 %pad_maximum_fusion = bf16[2048,4224]{1,0:T(8,128)(2,1)} fusion(bf16[2048,1408]{1,0:T(8,128)(2,1)} %fusion.6, bf16[2048,2816]{1,0:T(8,128)(2,1)S(1)} %bitcast_convert_fusion), kind=kLoop, calls=%fused_computation.3 | loop fusion | flops 34603008 | bytes 34603008 | tf_op jit(solution)/shard_map/concatenate | solution.py:450
  466.0 1.5 copy-done.49
  467.4 5.9 fusion.7
  474.4 1.5 copy.146
  476.0 6.2 all-to-all-start.9
  482.4 26.2 %all-reduce.2 = (bf16[128]{0:T(256)(128)(2,1)S(1)}, f32[2,256]{1,0:T(2,128)S(1)}) all-reduce(f32[128]{0:T(128)S(1)} %reduce_sum.109, f32[2,256]{1,0:T(2,128)S(1)} %broadcast_multiply_fusion), channel_id=1, replica_groups=mesh['seq'=32,'head'=4] {'head'}, use_global_device_ids=true, to_apply=%region_13.0 | all-reduce | flops 640 | bytes 4864 | tf_op jit(solution)/shard_map/psum | solution.py:533
  508.6 3.0 convert_reduce_fusion
  511.7 3.2 fusion.58
  514.9 125.8 %psum.23 = bf16[15,512]{1,0:T(8,128)(2,1)S(1)} all-reduce(bf16[15,512]{1,0:T(8,128)(2,1)S(1)} %fusion.65), channel_id=1, replica_groups=mesh['seq'=32,'head'=4] {'seq'}, use_global_device_ids=true, to_apply=%region_14.15 | all-reduce | flops 7680 | bytes 30720 | tf_op jit(solution)/shard_map/psum | solution.py:563
  642.6 1.3 copy.134
  (197 shorter events, 35.3 us)
Async XLA Ops:
  7.2 157.8 %copy-start = (bf16[512,2048]{1,0:T(8,128)(2,1)S(1)}, bf16[512,2048]{1,0:T(8,128)(2,1)}, u32[]{:S(2)}) copy-start(bf16[512,2048]{1,0:T(8,128)(2,1)} %param.19) | copy-start | bytes 6291460
  7.2 7.6 %copy-start.67 = (s32[2]{0:T(128)S(1)}, s32[2]{0:T(128)}, u32[]{:S(2)}) copy-start(s32[2]{0:T(128)} %param.13) | copy-start | bytes 28
  10.0 30.0 %all-to-all-start = ((bf16[4,2,256,512]{3,2,1,0:T(8,128)(2,1)}), bf16[4,2,256,512]{3,2,1,0:T(8,128)(2,1)}, u32[]{:S(2)}, u32[]{:S(2)}) async-start(bf16[4,2,256,512]{3,2,1,0:T(8,128)(2,1)} %broadcast_in_dim.17), calls=%async_computation | async-start | bytes 4194304 | tf_op jit(solution)/shard_map/all_to_all | solution.py:321
  44.1 2.2 copy-start.32
  49.3 313.6 %copy-start.56 = (f32[2,256]{1,0:T(2,128)}, f32[2,256]{1,0:T(2,128)S(1)}, u32[]{:S(2)}) copy-start(f32[2,256]{1,0:T(2,128)S(1)} %get-tuple-element.118) | copy-start | bytes 6148
  49.3 5.4 copy-start.54
  57.3 8.6 %copy-start.40 = (bf16[2,256,2048]{2,1,0:T(8,128)(2,1)}, bf16[2,256,2048]{2,1,0:T(8,128)(2,1)S(1)}, u32[]{:S(2)}) copy-start(bf16[2,256,2048]{2,1,0:T(8,128)(2,1)S(1)} %multiply_convert_fusion.2) | copy-start | bytes 6291460
  57.3 8.6 %copy-start.64 = (bf16[2048,4]{0,1:T(4,128)(2,1)S(1)}, bf16[2048,4]{0,1:T(4,128)(2,1)}, u32[]{:S(2)}) copy-start(bf16[2048,4]{0,1:T(4,128)(2,1)} %param.16) | copy-start | bytes 49156
  64.3 2.4 copy-start.42
  64.3 2.4 copy-start.28
  64.4 2.3 collective-permute-start
  66.7 40.3 %copy-start.16 = (f32[2,256,4]{2,1,0:T(8,128)}, f32[2,256,4]{2,1,0:T(8,128)S(1)}, u32[]{:S(2)}) copy-start(f32[2,256,4]{2,1,0:T(8,128)S(1)} %fusion.52.strength_ref) | copy-start | bytes 24580
  107.0 31.8 %copy-start.20 = (bf16[8,2,128,128]{3,2,1,0:T(8,128)(2,1)}, bf16[8,2,128,128]{3,2,1,0:T(8,128)(2,1)S(1)}, u32[]{:S(2)}) copy-start(bf16[8,2,128,128]{3,2,1,0:T(8,128)(2,1)S(1)} %get-tuple-element.42.inv_ref) | copy-start | bytes 1572868
  107.0 31.8 %copy-start.26 = (bf16[8,256,128]{2,1,0:T(8,128)(2,1)}, bf16[8,256,128]{2,1,0:T(8,128)(2,1)S(1)}, u32[]{:S(2)}) copy-start(bf16[8,256,128]{2,1,0:T(8,128)(2,1)S(1)} %get-tuple-element.33.u_ref) | copy-start | bytes 1572868
  107.0 50.3 %copy-start.29 = (f32[128]{0:T(128)S(1)}, f32[128]{0:T(128)}, u32[]{:S(2)}) copy-start(f32[128]{0:T(128)} %param.18) | copy-start | bytes 1540
  143.7 13.5 %all-to-all-start.2 = ((bf16[32,32,128]{2,1,0:T(8,128)(2,1)}), bf16[32,32,128]{2,1,0:T(8,128)(2,1)}, u32[]{:S(2)}, u32[]{:S(2)}) async-start(bf16[32,32,128]{2,1,0:T(8,128)(2,1)} %copy-done.13), calls=%async_computation.2 | async-start | bytes 524288 | tf_op jit(solution)/shard_map/all_to_all | solution.py:321
  166.5 31.2 %copy-start.43 = (bf16[2,256,512]{2,1,0:T(8,128)(2,1)S(1)}, bf16[2,256,512]{2,1,0:T(8,128)(2,1)}, u32[]{:S(2)}) copy-start(bf16[2,256,512]{2,1,0:T(8,128)(2,1)} %param.12) | copy-start | bytes 1572868
  199.4 43.5 %all-to-all-start.4 = ((bf16[4,2,256,512]{3,2,1,0:T(8,128)(2,1)}), bf16[4,2,256,512]{3,2,1,0:T(8,128)(2,1)}, u32[]{:S(2)}, u32[]{:S(2)}) async-start(bf16[4,2,256,512]{3,2,1,0:T(8,128)(2,1)} %broadcast_in_dim.19), calls=%async_computation.4 | async-start | bytes 4194304 | tf_op jit(solution)/shard_map/all_to_all | solution.py:321
  205.2 55.2 %all-gather.2.cloned.1.call-start = ((), (), s32[]{:S(2)}) async-start(), calls=%async_computation.14 | async-start | bytes 2621440 | tf_op jit(solution)/shard_map/all_gather | solution.py:370
  245.0 4.2 copy-start.55
  245.5 3.6 copy-start.33
  249.1 95.5 %copy-start.58 = (f32[2,256]{1,0:T(2,128)}, f32[2,256]{1,0:T(2,128)S(1)}, u32[]{:S(2)}) copy-start(f32[2,256]{1,0:T(2,128)S(1)} %get-tuple-element.119) | copy-start | bytes 6148
  249.1 95.5 %copy-start.60 = (f32[2,256]{1,0:T(2,128)}, f32[2,256]{1,0:T(2,128)S(1)}, u32[]{:S(2)}) copy-start(f32[2,256]{1,0:T(2,128)S(1)} %get-tuple-element.120) | copy-start | bytes 6148
  270.8 10.1 %copy-start.50 = (bf16[1,2,256,1408]{3,2,1,0:T(8,128)(2,1)}, bf16[1,2,256,1408]{3,2,1,0:T(8,128)(2,1)S(1)}, u32[]{:S(2)}) copy-start(bf16[1,2,256,1408]{3,2,1,0:T(8,128)(2,1)S(1)} %get-tuple-element.108) | copy-start | bytes 4325380
  270.8 10.1 %copy-start.52 = (bf16[1,2,256,1408]{3,2,1,0:T(8,128)(2,1)}, bf16[1,2,256,1408]{3,2,1,0:T(8,128)(2,1)S(1)}, u32[]{:S(2)}) copy-start(bf16[1,2,256,1408]{3,2,1,0:T(8,128)(2,1)S(1)} %get-tuple-element.109) | copy-start | bytes 4325380
  308.7 30.0 %all-to-all-start.6 = ((bf16[4,2,256,512]{3,2,1,0:T(8,128)(2,1)}), bf16[4,2,256,512]{3,2,1,0:T(8,128)(2,1)}, u32[]{:S(2)}, u32[]{:S(2)}) async-start(bf16[4,2,256,512]{3,2,1,0:T(8,128)(2,1)} %broadcast_in_dim.20), calls=%async_computation.7 | async-start | bytes 4194304 | tf_op jit(solution)/shard_map/all_to_all | solution.py:321
  314.6 197.1 %reduce-scatter.6.cloned.1.call-start = ((), (), s32[]{:S(2)}) async-start(), calls=%async_computation.13 | async-start | bytes 2621440 | tf_op jit(solution)/shard_map/reduce_scatter | solution.py:436
  341.8 2.9 copy-start.62
  344.0 2.2 copy-start.34
  344.0 2.9 copy-start.47
  348.1 1.4 copy-start.48
  348.1 1.7 copy-start.4
  348.1 1.9 copy-start.6
  348.1 2.1 copy-start.9
  348.1 2.2 copy-start.12
  348.1 2.6 copy-start.15
  355.5 16.3 %all-to-all-start.7 = ((bf16[32,32,128]{2,1,0:T(8,128)(2,1)}), bf16[32,32,128]{2,1,0:T(8,128)(2,1)S(1)}, u32[]{:S(2)}, u32[]{:S(2)}) async-start(bf16[32,32,128]{2,1,0:T(8,128)(2,1)} %bitcast.26), calls=%async_computation.8 | async-start | bytes 524288 | tf_op jit(solution)/shard_map/all_to_all | solution.py:321
  377.2 12.8 %all-to-all-start.8 = ((bf16[32,32,128]{2,1,0:T(8,128)(2,1)}), bf16[32,32,128]{2,1,0:T(8,128)(2,1)S(1)}, u32[]{:S(2)}, u32[]{:S(2)}) async-start(bf16[32,32,128]{2,1,0:T(8,128)(2,1)} %shard_map.207), calls=%async_computation.9 | async-start | bytes 524288 | tf_op jit(solution)/shard_map/all_to_all | solution.py:321
  381.1 8.9 %copy-start.17 = (f32[2,256,4]{2,1,0:T(8,128)S(1)}, f32[2,256,4]{2,1,0:T(8,128)}, u32[]{:S(2)}) copy-start(f32[2,256,4]{2,1,0:T(8,128)} %copy-done.16) | copy-start | bytes 24580
  381.1 8.9 %copy-start.19 = (bf16[8,3,128,128]{3,2,1,0:T(8,128)(2,1)S(1)}, bf16[8,3,128,128]{3,2,1,0:T(8,128)(2,1)}, u32[]{:S(2)}) copy-start(bf16[8,3,128,128]{3,2,1,0:T(8,128)(2,1)} %copy-done.18) | copy-start | bytes 2359300
  381.1 8.9 %copy-start.21 = (bf16[8,2,128,128]{3,2,1,0:T(8,128)(2,1)S(1)}, bf16[8,2,128,128]{3,2,1,0:T(8,128)(2,1)}, u32[]{:S(2)}) copy-start(bf16[8,2,128,128]{3,2,1,0:T(8,128)(2,1)} %copy-done.20) | copy-start | bytes 1572868
  381.1 261.5 %reduce-scatter.10.cloned.1.call-start = ((), (), s32[]{:S(2)}) async-start(), calls=%async_computation.16 | async-start | bytes 9191424
  392.1 13.2 %copy-start.41 = (bf16[2,256,2048]{2,1,0:T(8,128)(2,1)S(1)}, bf16[2,256,2048]{2,1,0:T(8,128)(2,1)}, u32[]{:S(2)}) copy-start(bf16[2,256,2048]{2,1,0:T(8,128)(2,1)} %copy-done.40) | copy-start | bytes 6291460
  404.0 3.1 collective-permute-start.1
  409.5 5.5 copy-start.46
  431.0 1.4 copy-start.51
  431.0 1.8 copy-start.53
  431.1 215.9 %reduce-scatter.8.cloned.1.call-start = ((), (), s32[]{:S(2)}) async-start(), calls=%async_computation.15 | async-start | bytes 17842176 | tf_op jit(solution)/shard_map/reduce_scatter | solution.py:453
  434.7 4.7 copy-start.68
  439.4 7.7 %copy-start.35 = (f32[4,2,32,8,512]{4,3,0,2,1:T(8,128)S(1)}, f32[4,2,32,8,512]{4,3,0,2,1:T(8,128)}, u32[]{:S(2)}) copy-start(f32[4,2,32,8,512]{4,3,0,2,1:T(8,128)} %copy-done.33) | copy-start | bytes 12582916
  439.4 7.7 %copy-start.61 = (f32[2,256]{1,0:T(2,128)S(1)}, f32[2,256]{1,0:T(2,128)}, u32[]{:S(2)}) copy-start(f32[2,256]{1,0:T(2,128)} %copy-done.60) | copy-start | bytes 6148
  465.9 1.5 copy-start.49
  467.4 5.9 copy-start.31
  467.4 5.9 copy-start.65
  476.0 35.7 %copy-start.37 = (f32[2,256,512]{2,1,0:T(8,128)S(1)}, f32[2,256,512]{2,1,0:T(8,128)}, u32[]{:S(2)}) copy-start(f32[2,256,512]{2,1,0:T(8,128)} %copy-done.36) | copy-start | bytes 3145732
  476.0 35.7 %copy-start.39 = (f32[2,256,512]{2,1,0:T(8,128)S(1)}, f32[2,256,512]{2,1,0:T(8,128)}, u32[]{:S(2)}) copy-start(f32[2,256,512]{2,1,0:T(8,128)} %copy-done.38) | copy-start | bytes 3145732
  476.0 35.7 %copy-start.44 = (bf16[2,256,512]{2,1,0:T(8,128)(2,1)S(1)}, bf16[2,256,512]{2,1,0:T(8,128)(2,1)}, u32[]{:S(2)}) copy-start(bf16[2,256,512]{2,1,0:T(8,128)(2,1)} %param.12) | copy-start | bytes 1572868
  476.0 35.7 %copy-start.57 = (f32[2,256]{1,0:T(2,128)S(1)}, f32[2,256]{1,0:T(2,128)}, u32[]{:S(2)}) copy-start(f32[2,256]{1,0:T(2,128)} %copy-done.56) | copy-start | bytes 6148
  476.0 35.7 %copy-start.59 = (f32[2,256]{1,0:T(2,128)S(1)}, f32[2,256]{1,0:T(2,128)}, u32[]{:S(2)}) copy-start(f32[2,256]{1,0:T(2,128)} %copy-done.58) | copy-start | bytes 6148
  476.0 35.7 %copy-start.63 = (f32[2,256]{1,0:T(2,128)S(1)}, f32[2,256]{1,0:T(2,128)}, u32[]{:S(2)}) copy-start(f32[2,256]{1,0:T(2,128)} %copy-done.62) | copy-start | bytes 6148
  476.0 35.7 %copy-start.66 = (f32[2,256]{1,0:T(2,128)S(1)}, f32[2,256]{1,0:T(2,128)}, u32[]{:S(2)}) copy-start(f32[2,256]{1,0:T(2,128)} %get-tuple-element.117) | copy-start | bytes 6148
  476.0 32.6 %all-to-all-start.9 = ((bf16[4,2,256,512]{3,2,1,0:T(8,128)(2,1)}), bf16[4,2,256,512]{3,2,1,0:T(8,128)(2,1)}, u32[]{:S(2)}, u32[]{:S(2)}) async-start(bf16[4,2,256,512]{3,2,1,0:T(8,128)(2,1)} %bitcast.202), calls=%async_computation.10 | async-start | bytes 4194304 | tf_op jit(solution)/shard_map/all_to_all | solution.py:321
  645.6 4.1 copy-start.1
  646.9 2.0 copy-start.45
  (18 other events, 18.1 us)
Sparse Core Ops, SparseCore 0:
  207.7 38.7 all-gather.1
  323.0 29.0 reduce-scatter.5
  431.2 94.9 reduce-scatter.9
  530.0 116.9 reduce-scatter.7
